TPU v7x, 32 devices: a whole 2x2x4 slice. The times are simulated.
32 devices in a mesh: section: 2 (over x), expert: 16 (over z, y, core).
Axes of the slice: x: 2, y: 2, z: 4, core: 2. Of those that a mesh axis runs over, the one named last changes fastest.
Arguments:
- histories: bfloat16 [2, 2048, 5120], P('section', 'expert'), may hold values from -6 to 6
- page_map: int32 [2, 2, 512], P('section', None, 'expert'), may hold values from 0 to 511, as said below
- user_pages: int32 [2, 16, 4], P('section', 'expert'), may hold values from 1 to 16, 32 in all within a row
- tails: int32 [2, 16, 4], P('section', 'expert'), may hold values from 1 to 4
- routes: int32 [2, 2048, 2], P('section', 'expert'), may hold values from 0 to 7, all different within a row; in each aligned block of 128 rows (0 to 127, 128 to 255, ..., all dimensions but the last counted through in order) at most 64 rows name the same one
- out_proj: bfloat16 [2, 1024, 1024], P('section', 'expert'), may hold values from -0.1875 to 0.1875
- router: bfloat16 [2, 1024, 8], P('section'), may hold values from -0.75 to 0.75
- w_gate: bfloat16 [2, 1024, 8192], P('section', None, 'expert'), may hold values from -0.1875 to 0.1875
- w_up: bfloat16 [2, 1024, 8192], P('section', None, 'expert'), may hold values from -0.1875 to 0.1875
- w_down: bfloat16 [2, 8192, 1024], P('section', 'expert'), may hold values from -0.1875 to 0.1875
Outputs:
- handed: bfloat16 [2, 2048, 1024], P('section', 'expert')
Inputs may be any that keep to these rules, and one draw needn't show every extreme that they name: page_map[0] is a permutation of the pages of a section and page_map[1] its inverse; every device holds exactly 32 pages before and after; no device's pages send more than 2 pages to one device, and some send exactly 2. `user_pages`: the 4 entries of one device sum to 32, and the largest is 16. `routes`: A row names 2 different experts; among the rows of one device, no expert is named more than 64 times, a bound that some block reaches.
All inputs are finite; a program needn't handle non-finite values.
Results may differ from a plain program's by a relative error of at most 0.012.
Values may be sent and summed in bfloat16 or wider, within the bound.
A program may use at most 64 MiB of HBM per device.

v0:
```python
import jax
import jax.numpy as jnp
from jax import lax
from jax.sharding import PartitionSpec as P

HEADS = 8


def swapped(shard, axis, apart):
    return lax.ppermute(shard, axis, [(i, i ^ 1 << apart) for i in range(lax.axis_size(axis))])


def from_behind(block, axis, distance):
    devices = range(lax.axis_size(axis))
    route = [((i - distance) % len(devices), i) for i in devices]
    return lax.ppermute(block, axis, route)


def layout_rows(counts, tail_rows, page_rows, row_count):
    starting = jnp.cumsum(counts) - counts
    length = (counts - 1) * page_rows + tail_rows
    row_index = jnp.arange(row_count, dtype=jnp.int32)
    page_of = row_index // page_rows
    owner_of = jnp.sum((starting[None, :] <= page_of[:, None]).astype(jnp.int32), axis=1) - 1
    member = owner_of[:, None] == jnp.arange(counts.shape[0], dtype=jnp.int32)[None, :]
    offset = jnp.sum(jnp.where(member, starting[None, :] * page_rows, 0), axis=1)
    spread = jnp.sum(jnp.where(member, length[None, :], 0), axis=1)
    return (owner_of, row_index - offset, spread)


def attend(balanced, counts, tail_rows, page_rows):
    row_count = balanced.shape[0]
    model_width = balanced.shape[1] // 5
    head_dim = model_width // HEADS
    owner_of, position, spread = layout_rows(counts, tail_rows, page_rows, row_count)
    allowed = (
        (owner_of[:, None] == owner_of[None, :])
        & (position[None, :] <= position[:, None])
        & (position[None, :] < spread[None, :])
    )
    queries = balanced[:, :model_width].reshape(row_count, HEADS, head_dim)
    key_rows = balanced[:, model_width : 2 * model_width].reshape(row_count, HEADS, head_dim)
    values = balanced[:, 2 * model_width : 3 * model_width].reshape(row_count, HEADS, head_dim)
    scores = jnp.einsum(
        "qhd,khd->hqk", queries, key_rows, preferred_element_type=jnp.float32
    ) * head_dim ** (-0.5)
    weights = (
        jnp.where(allowed[None], jax.nn.silu(scores), 0.0)
        / spread.astype(jnp.float32)[None, :, None]
    )
    weights = weights.astype(jnp.bfloat16)
    attended = jnp.einsum(
        "hqk,khd->qhd", weights, values, preferred_element_type=jnp.float32
    ).reshape(row_count, model_width)
    average = jnp.mean(attended, axis=1, keepdims=True)
    centered = attended - average
    variance = jnp.mean(centered * centered, axis=1, keepdims=True)
    gating = balanced[:, 3 * model_width : 4 * model_width].astype(jnp.float32)
    return (centered * lax.rsqrt(variance + 1e-05) * gating).astype(jnp.bfloat16)


def gate_share(normed, router, routes):
    logits = jnp.dot(normed, router, preferred_element_type=jnp.float32)
    scores = jax.nn.sigmoid(logits)
    picked = routes[:, :, None] == jnp.arange(router.shape[1], dtype=jnp.int32)[None, None, :]
    chosen = jnp.sum(jnp.where(picked, scores[:, None, :], 0.0), axis=2)
    return chosen / jnp.sum(chosen, axis=1, keepdims=True)


def slot_table(routes, experts, capacity):
    pair_count = routes.shape[0] * routes.shape[1]
    chosen = routes.reshape(-1)
    onehot = (chosen[:, None] == jnp.arange(experts, dtype=jnp.int32)[None, :]).astype(jnp.int32)
    before = jnp.cumsum(onehot, axis=0) - onehot
    ranking = jnp.sum(before * onehot, axis=1)
    slot_of_pair = chosen * capacity + ranking
    matches = slot_of_pair[None, :] == jnp.arange(experts * capacity, dtype=jnp.int32)[:, None]
    source_token = (
        jnp.sum(jnp.where(matches, jnp.arange(pair_count, dtype=jnp.int32)[None, :], 0), axis=1)
        // 2
    )
    return (slot_of_pair, source_token)


def whole_expert(incoming, gate_full, up_full, down_full):
    flat_rows = incoming.reshape(-1, incoming.shape[-1])
    gate_act = jnp.dot(flat_rows, gate_full, preferred_element_type=jnp.float32)
    up_act = jnp.dot(flat_rows, up_full, preferred_element_type=jnp.float32)
    hidden = (jax.nn.silu(gate_act) * up_act).astype(jnp.bfloat16)
    half_units = gate_full.shape[1] // 2
    first_part = jnp.dot(
        hidden[:, :half_units], down_full[:half_units], preferred_element_type=jnp.float32
    ).astype(jnp.bfloat16)
    second_part = jnp.dot(
        hidden[:, half_units:], down_full[half_units:], preferred_element_type=jnp.float32
    ).astype(jnp.bfloat16)
    summed = (first_part.astype(jnp.float32) + second_part.astype(jnp.float32)).astype(jnp.bfloat16)
    return summed.reshape(incoming.shape)


def shards(histories, page_map, user_pages, tails, routes, out_proj, router, w_gate, w_up, w_down):
    devices = lax.axis_size("expert")
    parity = lax.axis_index("expert") % 2
    row_count = histories.shape[1]
    stacked_width = histories.shape[2]
    model_width = stacked_width // 5
    pages_dev = page_map.shape[2]
    page_rows = row_count // pages_dev
    page_slots = (pages_dev + devices - 1) // devices
    page_block = histories[0].reshape(pages_dev, page_rows, stacked_width)
    target = page_map[0, 0]
    target_dev = target // pages_dev
    earlier = (target_dev[None, :] == target_dev[:, None]) & (target[None, :] < target[:, None])
    position = target_dev * page_slots + jnp.sum(earlier.astype(jnp.int32), axis=1)
    matches = position[None, :] == jnp.arange(devices * page_slots, dtype=jnp.int32)[:, None]
    chosen_page = jnp.sum(
        jnp.where(matches, jnp.arange(pages_dev, dtype=jnp.int32)[None, :], 0), axis=1
    )
    outgoing = page_block[chosen_page].reshape(devices, page_slots * page_rows, stacked_width)
    arrived = lax.all_to_all(outgoing, "expert", split_axis=0, concat_axis=0, tiled=True)
    anchor = page_map[0, 1]
    anchor_dev = anchor // pages_dev
    ordering = jnp.arange(pages_dev, dtype=jnp.int32)
    sooner = (anchor_dev[None, :] == anchor_dev[:, None]) & (ordering[None, :] < ordering[:, None])
    where_from = anchor_dev * page_slots + jnp.sum(sooner.astype(jnp.int32), axis=1)
    balanced = arrived.reshape(devices * page_slots, page_rows, stacked_width)[where_from].reshape(
        row_count, stacked_width
    )
    mixed_in = attend(balanced, user_pages[0, 0], tails[0, 0], page_rows)
    projected = jnp.dot(
        mixed_in,
        lax.all_gather(out_proj, "expert", axis=1, tiled=True)[0],
        preferred_element_type=jnp.float32,
    )
    resid = (balanced[:, 4 * model_width :].astype(jnp.float32) + projected).astype(jnp.bfloat16)
    resid_wide = resid.astype(jnp.float32)
    normed = (
        resid_wide * lax.rsqrt(jnp.mean(resid_wide * resid_wide, axis=1, keepdims=True) + 1e-06)
    ).astype(jnp.bfloat16)
    experts = router.shape[2]
    capacity = 4 * row_count // experts
    share = gate_share(normed, router[0], routes[0])
    slot_of_pair, source_token = slot_table(routes[0], experts, capacity)
    packed = normed[source_token].reshape(experts, capacity, model_width)
    is_odd = parity == 1
    half_units = w_gate.shape[2]
    gate_up = jnp.concatenate([w_gate[0], w_up[0]], axis=1)
    other_gate_up = swapped(gate_up, "expert", 0)
    other_down = swapped(w_down[0], "expert", 0)
    own_gate = gate_up[:, :half_units]
    own_up = gate_up[:, half_units:]
    other_gate = other_gate_up[:, :half_units]
    other_up = other_gate_up[:, half_units:]
    gate_full = jnp.where(
        is_odd,
        jnp.concatenate([other_gate, own_gate], axis=1),
        jnp.concatenate([own_gate, other_gate], axis=1),
    )
    up_full = jnp.where(
        is_odd,
        jnp.concatenate([other_up, own_up], axis=1),
        jnp.concatenate([own_up, other_up], axis=1),
    )
    down_full = jnp.where(
        is_odd,
        jnp.concatenate([other_down, w_down[0]], axis=0),
        jnp.concatenate([w_down[0], other_down], axis=0),
    )
    half_cap = capacity // 2
    sent_rows = packed.reshape(experts * 2, half_cap, model_width)
    own_rows = lax.all_to_all(sent_rows, "expert", split_axis=0, concat_axis=0, tiled=True)
    served = whole_expert(own_rows, gate_full, up_full, down_full)
    came_back = lax.all_to_all(served, "expert", split_axis=0, concat_axis=0, tiled=True)
    result = came_back.reshape(experts, capacity, model_width)
    picked = result.reshape(experts * capacity, model_width)[slot_of_pair]
    picked = picked.reshape(row_count, 2, model_width).astype(jnp.float32)
    mixture = jnp.sum(picked * share[:, :, None], axis=1)
    output_rows = (resid_wide + mixture).astype(jnp.bfloat16)
    return from_behind(output_rows[None], "section", 1)


def solution(mesh):
    in_specs = (
        P("section", "expert", None),
        P("section", None, "expert"),
        P("section", "expert", None),
        P("section", "expert", None),
        P("section", "expert", None),
        P("section", "expert", None),
        P("section", None, None),
        P("section", None, "expert"),
        P("section", None, "expert"),
        P("section", "expert", None),
    )
    out_specs = P("section", "expert", None)
    return jax.shard_map(shards, mesh=mesh, in_specs=in_specs, out_specs=out_specs, check_vma=False)
```

profile of v0, /device:TPU:9, one launch (start us, length us, event | category | flops | bytes accessed | tf_op | source)
XLA Modules:
  0.0 166.5 jit_solution(6720429883155429973)
XLA Ops:
  8.3 2.6 %reshape_squeeze.6 = bf16[32,4,5120]{2,1,0:T(4,128)(2,1)S(1)} reshape(bf16[1,128,5120]{2,1,0:T(8,128)(2,1)} %param.10) | data formatting | bytes 2621440 | tf_op jit(solution)/shard_map/reshape;squeeze | solution.py:110
  10.9 1.7 %gather_fusion = bf16[32,4,5120]{2,1,0:T(4,128)(2,1)S(1)} fusion(bf16[32,4,5120]{2,1,0:T(4,128)(2,1)S(1)} %reshape_squeeze.6, s32[1024]{0:T(1024)S(1)} %pad_clamp_fusion.3), kind=kCustom, calls=%fused_computation | custom fusion | bytes 2621568 | tf_op jit(solution)/shard_map/gather | solution.py:119
  12.6 1.3 reshape.553
  13.9 6.6 %all-to-all-start = ((bf16[16,8,5120]{2,1,0:T(8,128)(2,1)}), bf16[16,8,5120]{2,1,0:T(8,128)(2,1)S(1)}, u32[]{:S(2)}, u32[]{:S(2)}) async-start(bf16[16,8,5120]{2,1,0:T(8,128)(2,1)} %reshape.553), calls=%async_computation | async-start | bytes 2621440 | tf_op jit(solution)/shard_map/all_to_all | solution.py:120
  21.3 1.6 pad_maximum_fusion.1
  25.4 29.5 %all-to-all-done = bf16[16,8,5120]{2,1,0:T(8,128)(2,1)S(1)} async-done(((bf16[16,8,5120]{2,1,0:T(8,128)(2,1)}), bf16[16,8,5120]{2,1,0:T(8,128)(2,1)S(1)}, u32[]{:S(2)}, u32[]{:S(2)}) %all-to-all-start) | async-done | bytes 1310752 | tf_op jit(solution)/shard_map/all_to_all | solution.py:120
  55.4 1.7 %gather_fusion.1 = bf16[32,4,5120]{2,1,0:T(4,128)(2,1)S(1)} fusion(bf16[32,4,5120]{2,1,0:T(4,128)(2,1)S(1)} %reshape.554, s32[1024]{0:T(1024)S(1)} %pad_clamp_fusion.2), kind=kCustom, calls=%fused_computation.1 | custom fusion | bytes 2621568 | tf_op jit(solution)/shard_map/gather | solution.py:126
  59.0 12.8 %all-gather.2.cloned.1.call-done = bf16[1,1024,1024]{2,1,0:T(8,128)(2,1)} async-done(((bf16[1,64,1024]{2,1,0:T(8,128)(2,1)}), bf16[1,1024,1024]{2,1,0:T(8,128)(2,1)}) %all-gather.2.cloned.1.call-update) | async-done | bytes 2097168 | tf_op jit(solution)/shard_map/all_gather | solution.py:132
  71.8 2.2 %multiply_reduce_fusion.1 = (f32[128]{0:T(128)S(1)}, f32[128,1024]{1,0:T(8,128)S(1)}) fusion(bf16[1,1024,1024]{2,1,0:T(8,128)(2,1)} %all-gather.2.cloned.1.call-done, f32[128,1024]{1,0:T(8,128)S(1)} %copy.31, bf16[128,5120]{1,0:T(8,128)(2,1)S(1)} %reshape.555, f32[128]{0:T(128)S(1)} %add_rsqrt_fusion.1, f32[128]{0:T(128)S(1)} %broadcast_multiply_fusion.1), kind=kOutput, calls=%fused_computation.48 | convolution fusion | flops 269877120 | bytes 3671552 | tf_op jit(solution)/shard_map/dot_general | solution.py:130
  74.1 2.8 %gather_fusion.2 = bf16[512,1024]{1,0:T(8,128)(2,1)} fusion(bf16[128,1024]{1,0:T(8,128)(2,1)S(1)} %multiply_convert_fusion.1, s32[1024]{0:T(1024)S(1)} %pad_clamp_fusion.1), kind=kCustom, calls=%fused_computation.2 | custom fusion | bytes 2099200 | tf_op jit(solution)/shard_map/gather | solution.py:144
  76.9 5.6 %all-to-all-start.1 = ((bf16[16,32,1024]{2,1,0:T(8,128)(2,1)}), bf16[16,32,1024]{2,1,0:T(8,128)(2,1)}, u32[]{:S(2)}, u32[]{:S(2)}) async-start(bf16[16,32,1024]{2,1,0:T(8,128)(2,1)} %bitcast.21), calls=%async_computation.1 | async-start | bytes 2097152 | tf_op jit(solution)/shard_map/all_to_all | solution.py:171
  83.0 2.4 %collective-permute-done.1 = bf16[512,1024]{1,0:T(8,128)(2,1)} collective-permute-done((bf16[512,1024]{1,0:T(8,128)(2,1)S(1)}, bf16[512,1024]{1,0:T(8,128)(2,1)}, u32[]{:S(2)}, u32[]{:S(2)}) %collective-permute-start.1) | collective-permute-done | bytes 1048608 | tf_op jit(solution)/shard_map/ppermute | solution.py:10
  85.4 3.5 %maximum_select_fusion = bf16[1024,1024]{1,0:T(8,128)(2,1)S(1)} fusion(bf16[512,1024]{1,0:T(8,128)(2,1)} %bitcast.101, bf16[512,1024]{1,0:T(8,128)(2,1)} %collective-permute-done.1, pred[]{:T(512)S(6)} %eq.153), kind=kLoop, calls=%fused_computation.19 | loop fusion | flops 9437184 | bytes 4194305 | tf_op jit(solution)/shard_map/jit(_where)/select_n | solution.py:164
  89.0 3.0 %fusion.62 = (bf16[1024,512]{1,0:T(8,128)(2,1)}, bf16[1024,512]{1,0:T(8,128)(2,1)}) fusion(bf16[1024,1024]{1,0:T(8,128)(2,1)} %collective-permute-done), kind=kLoop, calls=%fused_computation.137 | loop fusion | bytes 4194304 | tf_op jit(solution)/shard_map/slice | solution.py:153
  91.9 15.6 %all-to-all-done.1 = bf16[16,32,1024]{2,1,0:T(8,128)(2,1)} async-done(((bf16[16,32,1024]{2,1,0:T(8,128)(2,1)}), bf16[16,32,1024]{2,1,0:T(8,128)(2,1)}, u32[]{:S(2)}, u32[]{:S(2)}) %all-to-all-start.1) | async-done | bytes 1048608 | tf_op jit(solution)/shard_map/all_to_all | solution.py:171
  107.5 4.1 %fusion.1 = f32[512,1024]{1,0:T(8,128)S(1)} fusion(bf16[512,1024]{1,0:T(8,128)(2,1)} %bitcast.22, bf16[1024,512]{1,0:T(8,128)(2,1)} %bitcast.104, bf16[1024,512]{1,0:T(8,128)(2,1)} %get-tuple-element.12, pred[]{:T(512)S(6)} %eq.153), kind=kOutput, calls=%fused_computation.8 | convolution fusion | flops 1083179008 | bytes 5242881 | tf_op jit(solution)/shard_map/dot_general | solution.py:87
  111.6 3.6 %multiply_convert_fusion = bf16[512,1024]{1,0:T(8,128)(2,1)S(1)} fusion(f32[512,1024]{1,0:T(8,128)S(1)} %fusion.1, bf16[512,1024]{1,0:T(8,128)(2,1)} %bitcast.22, bf16[1024,512]{1,0:T(8,128)(2,1)S(1)} %bitcast.107, bf16[1024,512]{1,0:T(8,128)(2,1)S(1)} %copy-done.5, pred[]{:T(512)S(6)} %eq.153), kind=kOutput, calls=%fused_computation.23 | convolution fusion | flops 1086324736 | bytes 6291457 | tf_op jit(solution)/shard_map/dot_general | solution.py:88
  116.0 1.7 %add_convert_fusion = bf16[512,1024]{1,0:T(8,128)(2,1)} fusion(bf16[512,1024]{1,0:T(8,128)(2,1)S(1)} %convolution_convert_fusion.1, bf16[1024,1024]{1,0:T(8,128)(2,1)S(1)} %maximum_select_fusion, bf16[512,1024]{1,0:T(8,128)(2,1)S(1)} %multiply_convert_fusion), kind=kOutput, calls=%fused_computation.22 | convolution fusion | flops 539492352 | bytes 3670016 | tf_op jit(solution)/shard_map/dot_general | solution.py:94
  117.7 4.9 %all-to-all-start.2 = ((bf16[16,32,1024]{2,1,0:T(8,128)(2,1)}), bf16[16,32,1024]{2,1,0:T(8,128)(2,1)S(1)}, u32[]{:S(2)}, u32[]{:S(2)}) async-start(bf16[16,32,1024]{2,1,0:T(8,128)(2,1)} %bitcast.103), calls=%async_computation.2 | async-start | bytes 2097152 | tf_op jit(solution)/shard_map/all_to_all | solution.py:173
  123.3 24.2 %all-to-all-done.2 = bf16[16,32,1024]{2,1,0:T(8,128)(2,1)S(1)} async-done(((bf16[16,32,1024]{2,1,0:T(8,128)(2,1)}), bf16[16,32,1024]{2,1,0:T(8,128)(2,1)S(1)}, u32[]{:S(2)}, u32[]{:S(2)}) %all-to-all-start.2) | async-done | bytes 1048608 | tf_op jit(solution)/shard_map/all_to_all | solution.py:173
  147.5 1.2 gather_fusion.3
  149.3 1.3 multiply_reduce_fusion
  150.7 1.2 collective-permute-start.2
  152.0 6.9 %collective-permute-done.2 = bf16[1,128,1024]{2,1,0:T(8,128)(2,1)S(1)} collective-permute-done((bf16[1,128,1024]{2,1,0:T(8,128)(2,1)S(1)}, bf16[1,128,1024]{2,1,0:T(8,128)(2,1)S(1)}, u32[]{:S(2)}, u32[]{:S(2)}) %collective-permute-start.2) | collective-permute-done | bytes 262176 | tf_op jit(solution)/shard_map/ppermute | solution.py:16
  (83 shorter events, 10.6 us)
Async XLA Ops:
  6.5 116.4 %copy-start = (bf16[1,1024,8]{1,2,0:T(8,128)(2,1)S(1)}, bf16[1,1024,8]{1,2,0:T(8,128)(2,1)}, u32[]{:S(2)}) copy-start(bf16[1,1024,8]{1,2,0:T(8,128)(2,1)} %param.16) | copy-start | bytes 49156
  12.6 8.6 %copy-start.2 = (bf16[1,1024,512]{2,1,0:T(8,128)(2,1)S(1)}, bf16[1,1024,512]{2,1,0:T(8,128)(2,1)}, u32[]{:S(2)}) copy-start(bf16[1,1024,512]{2,1,0:T(8,128)(2,1)} %param.17) | copy-start | bytes 3145732
  12.6 8.6 %copy-start.3 = (bf16[1,1024,512]{2,1,0:T(8,128)(2,1)S(1)}, bf16[1,1024,512]{2,1,0:T(8,128)(2,1)}, u32[]{:S(2)}) copy-start(bf16[1,1024,512]{2,1,0:T(8,128)(2,1)} %param.18) | copy-start | bytes 3145732
  13.9 41.0 %all-to-all-start = ((bf16[16,8,5120]{2,1,0:T(8,128)(2,1)}), bf16[16,8,5120]{2,1,0:T(8,128)(2,1)S(1)}, u32[]{:S(2)}, u32[]{:S(2)}) async-start(bf16[16,8,5120]{2,1,0:T(8,128)(2,1)} %reshape.553), calls=%async_computation | async-start | bytes 2621440 | tf_op jit(solution)/shard_map/all_to_all | solution.py:120
  20.5 51.4 %all-gather.2.cloned.1.call-start = ((), (), s32[]{:S(2)}) async-start(), calls=%async_computation.3 | async-start | bytes 2228224 | tf_op jit(solution)/shard_map/all_gather | solution.py:132
  21.2 2.0 %copy-start.6 = (s32[1,128,2]{1,2,0:T(2,128)S(1)}, s32[1,128,2]{1,2,0:T(2,128)}, u32[]{:S(2)}) copy-start(s32[1,128,2]{1,2,0:T(2,128)} %param.14) | copy-start | bytes 3076
  21.2 2.4 %copy-start.8 = (s32[1,1,4]{2,1,0:T(1,128)S(1)}, s32[1,1,4]{2,1,0:T(1,128)}, u32[]{:S(2)}) copy-start(s32[1,1,4]{2,1,0:T(1,128)} %param.12) | copy-start | bytes 52
  21.3 2.6 %copy-start.9 = (s32[1,1,4]{2,1,0:T(1,128)S(1)}, s32[1,1,4]{2,1,0:T(1,128)}, u32[]{:S(2)}) copy-start(s32[1,1,4]{2,1,0:T(1,128)} %param.13) | copy-start | bytes 52
  21.3 3.6 %copy-start.7 = (s32[1,2,32]{2,1,0:T(2,128)S(1)}, s32[1,2,32]{2,1,0:T(2,128)}, u32[]{:S(2)}) copy-start(s32[1,2,32]{2,1,0:T(2,128)} %param.11) | copy-start | bytes 772
  22.9 66.0 %collective-permute-start = (bf16[1024,1024]{1,0:T(8,128)(2,1)}, bf16[1024,1024]{1,0:T(8,128)(2,1)}, u32[]{:S(2)}, u32[]{:S(2)}) collective-permute-start(bf16[1024,1024]{1,0:T(8,128)(2,1)} %pad_maximum_fusion.1), channel_id=1, source_target_pairs={{0,1},{1,0},{2,3},{3,2},{4,5},{5,4},{6,7},{7,6},{8,9},{9,8},{10,11... | collective-permute-start | bytes 6291464 | tf_op jit(solution)/shard_map/ppermute | solution.py:10
  76.9 5.6 %copy-start.1 = (bf16[1,512,1024]{2,1,0:T(8,128)(2,1)S(1)}, bf16[1,512,1024]{2,1,0:T(8,128)(2,1)}, u32[]{:S(2)}) copy-start(bf16[1,512,1024]{2,1,0:T(8,128)(2,1)} %param.19) | copy-start | bytes 3145732
  76.9 30.6 %all-to-all-start.1 = ((bf16[16,32,1024]{2,1,0:T(8,128)(2,1)}), bf16[16,32,1024]{2,1,0:T(8,128)(2,1)}, u32[]{:S(2)}, u32[]{:S(2)}) async-start(bf16[16,32,1024]{2,1,0:T(8,128)(2,1)} %bitcast.21), calls=%async_computation.1 | async-start | bytes 2097152 | tf_op jit(solution)/shard_map/all_to_all | solution.py:171
  82.6 2.9 %collective-permute-start.1 = (bf16[512,1024]{1,0:T(8,128)(2,1)S(1)}, bf16[512,1024]{1,0:T(8,128)(2,1)}, u32[]{:S(2)}, u32[]{:S(2)}) collective-permute-start(bf16[512,1024]{1,0:T(8,128)(2,1)S(1)} %bitcast.102), channel_id=1, source_target_pairs={{0,1},{1,0},{2,3},{3,2},{4,5},{5,4},{6,7},{7,6},{8,9},{9,8},{10,11... | collective-permute-start | bytes 3145736 | tf_op jit(solution)/shard_map/ppermute | solution.py:10
  107.5 4.1 %copy-start.4 = (bf16[1,1024,512]{2,1,0:T(8,128)(2,1)S(1)}, bf16[1,1024,512]{2,1,0:T(8,128)(2,1)}, u32[]{:S(2)}) copy-start(bf16[1,1024,512]{2,1,0:T(8,128)(2,1)} %param.18) | copy-start | bytes 3145732
  107.5 4.1 %copy-start.5 = (bf16[1024,512]{1,0:T(8,128)(2,1)S(1)}, bf16[1024,512]{1,0:T(8,128)(2,1)}, u32[]{:S(2)}) copy-start(bf16[1024,512]{1,0:T(8,128)(2,1)} %get-tuple-element.11) | copy-start | bytes 3145732
  117.7 29.8 %all-to-all-start.2 = ((bf16[16,32,1024]{2,1,0:T(8,128)(2,1)}), bf16[16,32,1024]{2,1,0:T(8,128)(2,1)S(1)}, u32[]{:S(2)}, u32[]{:S(2)}) async-start(bf16[16,32,1024]{2,1,0:T(8,128)(2,1)} %bitcast.103), calls=%async_computation.2 | async-start | bytes 2097152 | tf_op jit(solution)/shard_map/all_to_all | solution.py:173
  150.7 8.2 %collective-permute-start.2 = (bf16[1,128,1024]{2,1,0:T(8,128)(2,1)S(1)}, bf16[1,128,1024]{2,1,0:T(8,128)(2,1)S(1)}, u32[]{:S(2)}, u32[]{:S(2)}) collective-permute-start(bf16[1,128,1024]{2,1,0:T(8,128)(2,1)S(1)} %fusion.39), channel_id=1, source_target_pairs={{16,0},{0,16},{17,1},{1,17},{18,2},{2,18},{19,3},{3,19},{20,4},{4,... | collective-permute-start | bytes 786440 | tf_op jit(solution)/shard_map/ppermute | solution.py:16
Sparse Core Ops, SparseCore 0:
  23.5 48.3 all-gather.1
where the time goes:
time: 167 us; the launch traced here: 166 us
  waiting for transfers between devices  92.2 us (55%)
  starting transfers between devices  19.2 us (11%)
  local copies, waits for them, and re-layouts  18.8 us (11%)
  between operations  13.8 us (8%)
  matrix products  13.1 us (8%)
  other arithmetic  9.38 us (6%)
    all_to_all x1, waiting for transfers between devices, shards(): lax.all_to_all(outgoing, 'expert', split_axis=0, concat_axis=0, tiled=True)  29.5 us
    all_to_all x1, waiting for transfers between devices, shards(): lax.all_to_all(served, 'expert', split_axis=0, concat_axis=0, tiled=True)  24.2 us
    all_to_all x1, waiting for transfers between devices, shards(): lax.all_to_all(sent_rows, 'expert', split_axis=0, concat_axis=0, tiled=True)  15.6 us
    all_gather x1, waiting for transfers between devices, shards(): lax.all_gather(out_proj, 'expert', axis=1, tiled=True)[0]  12.8 us
    ppermute x1, waiting for transfers between devices, from_behind(): return lax.ppermute(block, axis, route)  6.94 us
    all_to_all x1, starting transfers between devices, shards(): lax.all_to_all(outgoing, 'expert', split_axis=0, concat_axis=0, tiled=True)  6.61 us
    all_to_all x1, starting transfers between devices, shards(): lax.all_to_all(sent_rows, 'expert', split_axis=0, concat_axis=0, tiled=True)  5.62 us
    all_to_all x1, starting transfers between devices, shards(): lax.all_to_all(served, 'expert', split_axis=0, concat_axis=0, tiled=True)  4.94 us
  transfers between devices with their start and end apart: 7, of which 6 were waited for; matrix products, arithmetic and copies ran while one was open for 12% of the time, Pallas kernels for 0%

commit v1 on v0

v1 whole, which is shorter than its diff:
```python
import jax
import jax.numpy as jnp
from jax import lax
from jax.sharding import PartitionSpec as P

HEADS = 8


def swapped(shard, axis, apart):
    return lax.ppermute(shard, axis, [(i, i ^ 1 << apart) for i in range(lax.axis_size(axis))])


def from_behind(block, axis, distance):
    devices = range(lax.axis_size(axis))
    route = [((i - distance) % len(devices), i) for i in devices]
    return lax.ppermute(block, axis, route)


def layout_rows(counts, tail_rows, page_rows, row_count):
    member_index = jnp.arange(counts.shape[0], dtype=jnp.int32)
    ahead = member_index[None, :] < member_index[:, None]
    starting = jnp.sum(jnp.where(ahead, counts[None, :], 0), axis=1)
    length = (counts - 1) * page_rows + tail_rows
    row_index = jnp.arange(row_count, dtype=jnp.int32)
    page_of = row_index // page_rows
    owner_of = jnp.sum((starting[None, :] <= page_of[:, None]).astype(jnp.int32), axis=1) - 1
    member = owner_of[:, None] == jnp.arange(counts.shape[0], dtype=jnp.int32)[None, :]
    offset = jnp.sum(jnp.where(member, starting[None, :] * page_rows, 0), axis=1)
    spread = jnp.sum(jnp.where(member, length[None, :], 0), axis=1)
    return (owner_of, row_index - offset, spread)


def attend(balanced, counts, tail_rows, page_rows):
    row_count = balanced.shape[0]
    model_width = balanced.shape[1] // 5
    head_dim = model_width // HEADS
    owner_of, position, spread = layout_rows(counts, tail_rows, page_rows, row_count)
    allowed = (
        (owner_of[:, None] == owner_of[None, :])
        & (position[None, :] <= position[:, None])
        & (position[None, :] < spread[None, :])
    )
    queries = balanced[:, :model_width].reshape(row_count, HEADS, head_dim)
    key_rows = balanced[:, model_width : 2 * model_width].reshape(row_count, HEADS, head_dim)
    values = balanced[:, 2 * model_width : 3 * model_width].reshape(row_count, HEADS, head_dim)
    scores = jnp.einsum(
        "qhd,khd->hqk", queries, key_rows, preferred_element_type=jnp.float32
    ) * head_dim ** (-0.5)
    weights = (
        jnp.where(allowed[None], jax.nn.silu(scores), 0.0)
        / spread.astype(jnp.float32)[None, :, None]
    )
    weights = weights.astype(jnp.bfloat16)
    attended = jnp.einsum(
        "hqk,khd->qhd", weights, values, preferred_element_type=jnp.float32
    ).reshape(row_count, model_width)
    average = jnp.mean(attended, axis=1, keepdims=True)
    centered = attended - average
    variance = jnp.mean(centered * centered, axis=1, keepdims=True)
    gating = balanced[:, 3 * model_width : 4 * model_width].astype(jnp.float32)
    return (centered * lax.rsqrt(variance + 1e-05) * gating).astype(jnp.bfloat16)


def gate_share(normed, router, routes):
    logits = jnp.dot(normed, router, preferred_element_type=jnp.float32)
    scores = jax.nn.sigmoid(logits)
    picked = routes[:, :, None] == jnp.arange(router.shape[1], dtype=jnp.int32)[None, None, :]
    chosen = jnp.sum(jnp.where(picked, scores[:, None, :], 0.0), axis=2)
    return chosen / jnp.sum(chosen, axis=1, keepdims=True)


def pair_slots(routes, capacity):
    chosen = routes.reshape(-1)
    order = jnp.arange(chosen.shape[0], dtype=jnp.int32)
    same = (chosen[:, None] == chosen[None, :]) & (order[None, :] < order[:, None])
    ranking = jnp.sum(same.astype(jnp.int32), axis=1)
    return (chosen * capacity + ranking).reshape(routes.shape)


def per_row(pages, page_rows):
    return jnp.broadcast_to(pages[:, None], (pages.shape[0], page_rows)).reshape(-1)


def half_expert(rows, gate_cols, up_cols, down_rows):
    gate_act = jnp.dot(rows, gate_cols, preferred_element_type=jnp.float32)
    up_act = jnp.dot(rows, up_cols, preferred_element_type=jnp.float32)
    hidden = (jax.nn.silu(gate_act) * up_act).astype(jnp.bfloat16)
    return jnp.dot(hidden, down_rows, preferred_element_type=jnp.float32).astype(jnp.bfloat16)


def gathered_projection(block):
    devices = lax.axis_size("expert")
    groups = [list(range(first, devices, 2)) for first in range(2)]
    own = lax.all_gather(block, "expert", axis_index_groups=groups)
    return own, swapped(own, "expert", 0)


def shards(histories, page_map, user_pages, tails, routes, out_proj, router, w_gate, w_up, w_down):
    devices = lax.axis_size("expert")
    parity = lax.axis_index("expert") % 2
    own_proj, other_proj = gathered_projection(out_proj[0])
    other_gate = swapped(w_gate[0], "expert", 0)
    other_up = swapped(w_up[0], "expert", 0)
    other_down = swapped(w_down[0], "expert", 0)
    row_count = histories.shape[1]
    stacked_width = histories.shape[2]
    model_width = stacked_width // 5
    pages_dev = page_map.shape[2]
    page_rows = row_count // pages_dev
    page_slots = (pages_dev + devices - 1) // devices
    target = page_map[0, 0]
    target_dev = target // pages_dev
    earlier = (target_dev[None, :] == target_dev[:, None]) & (target[None, :] < target[:, None])
    position = target_dev * page_slots + jnp.sum(earlier.astype(jnp.int32), axis=1)
    sent_count = devices * page_slots * page_rows
    source_row = jnp.arange(row_count, dtype=jnp.int32)
    wire_row = jnp.arange(sent_count, dtype=jnp.int32)
    goes_to = per_row(position, page_rows) * page_rows + source_row % page_rows
    placing = (wire_row[:, None] == goes_to[None, :]).astype(jnp.bfloat16)
    outgoing = jnp.dot(placing, histories[0])
    arrived = lax.all_to_all(outgoing, "expert", split_axis=0, concat_axis=0, tiled=True)
    anchor = page_map[0, 1]
    anchor_dev = anchor // pages_dev
    ordering = jnp.arange(pages_dev, dtype=jnp.int32)
    sooner = (anchor_dev[None, :] == anchor_dev[:, None]) & (ordering[None, :] < ordering[:, None])
    where_from = anchor_dev * page_slots + jnp.sum(sooner.astype(jnp.int32), axis=1)
    comes_from = per_row(where_from, page_rows) * page_rows + source_row % page_rows
    taking = (comes_from[:, None] == wire_row[None, :]).astype(jnp.bfloat16)
    balanced = jnp.dot(taking, arrived)
    mixed_in = attend(balanced, user_pages[0, 0], tails[0, 0], page_rows)
    is_odd = parity == 1
    even_odd = mixed_in.reshape(row_count, devices // 2, 2, out_proj.shape[1])
    even = even_odd[:, :, 0].reshape(row_count, -1)
    odd = even_odd[:, :, 1].reshape(row_count, -1)
    own_mixed = jnp.where(is_odd, odd, even)
    other_mixed = jnp.where(is_odd, even, odd)
    projected = jnp.dot(
        own_mixed, own_proj.reshape(-1, model_width), preferred_element_type=jnp.float32
    ) + jnp.dot(
        other_mixed, other_proj.reshape(-1, model_width), preferred_element_type=jnp.float32
    )
    resid = (balanced[:, 4 * model_width :].astype(jnp.float32) + projected).astype(jnp.bfloat16)
    resid_wide = resid.astype(jnp.float32)
    normed = (
        resid_wide * lax.rsqrt(jnp.mean(resid_wide * resid_wide, axis=1, keepdims=True) + 1e-06)
    ).astype(jnp.bfloat16)
    experts = router.shape[2]
    capacity = 4 * row_count // experts
    share = gate_share(normed, router[0], routes[0])
    slots = pair_slots(routes[0], capacity)
    slot_index = jnp.arange(experts * capacity, dtype=jnp.int32)
    packing = (
        (slots[None, :, 0] == slot_index[:, None]) | (slots[None, :, 1] == slot_index[:, None])
    ).astype(jnp.bfloat16)
    packed = jnp.dot(packing, normed)
    own_rows = lax.all_to_all(packed, "expert", split_axis=0, concat_axis=0, tiled=True)
    own_part = half_expert(own_rows, w_gate[0], w_up[0], w_down[0])
    other_part = half_expert(own_rows, other_gate, other_up, other_down)
    served = (own_part.astype(jnp.float32) + other_part.astype(jnp.float32)).astype(jnp.bfloat16)
    came_back = lax.all_to_all(served, "expert", split_axis=0, concat_axis=0, tiled=True)
    mixture = jnp.zeros_like(resid_wide)
    for k in range(slots.shape[1]):
        picking = (slots[:, k : k + 1] == slot_index[None, :]).astype(jnp.bfloat16)
        picked = jnp.dot(picking, came_back, preferred_element_type=jnp.float32)
        mixture = mixture + picked * share[:, k : k + 1]
    output_rows = (resid_wide + mixture).astype(jnp.bfloat16)
    return from_behind(output_rows[None], "section", 1)


def solution(mesh):
    in_specs = (
        P("section", "expert", None),
        P("section", None, "expert"),
        P("section", "expert", None),
        P("section", "expert", None),
        P("section", "expert", None),
        P("section", "expert", None),
        P("section", None, None),
        P("section", None, "expert"),
        P("section", None, "expert"),
        P("section", "expert", None),
    )
    out_specs = P("section", "expert", None)
    return jax.shard_map(shards, mesh=mesh, in_specs=in_specs, out_specs=out_specs, check_vma=False)
```

time: 167 us -> 166 us (level)
  local copies, waits for them, and re-layouts: 18.8 us -> 4.04 us
  waiting for transfers between devices: 92.2 us -> 103 us
  matrix products: 13.1 us -> 21.8 us
  other arithmetic: 9.38 us -> 3.09 us
    all_gather x1, waiting for transfers between devices: 12.8 us -> 46.8 us  [gathered_projection(): own = lax.all_gather(block, 'expert', axis_index_groups=groups)]
    all_to_all x1, waiting for transfers between devices: 29.5 us -> 0.01 us  [shards(): lax.all_to_all(outgoing, 'expert', split_axis=0, concat_axis=0, tiled=True)]
    dot_general x5 -> x11, matrix products: 12.3 us -> 20.9 us  [the longest x2 8.7 us: half_expert(): jnp.dot(hidden, down_rows, preferred_element_type=jnp.float32)]
    all_to_all x1, waiting for transfers between devices: 15.6 us -> 24 us  [shards(): lax.all_to_all(packed, 'expert', split_axis=0, concat_axis=0, tiled=True)]
    gather x4 -> x0, local copies, waits for them, and re-layouts: 7.31 us -> none  [the longest x1 2.79 us: shards(): packed = normed[source_token].reshape(experts, capacity, model_width)]
    slice x6 -> x1, local copies, waits for them, and re-layouts: 3.76 us -> 0.17 us  [shards(): picking = (slots[:, k:k + 1] == slot_index[None, :]).astype(jnp.bfloat16)]
    select_n x5 -> x1, other arithmetic: 3.58 us -> 0.02 us  [shards(): other_mixed = jnp.where(is_odd, even, odd)]
    another operation x3 -> x1, local copies, waits for them, and re-layouts: 2.72 us -> 0.06 us  [pair_slots(): chosen = routes.reshape(-1)]
  transfers between devices with their start and end apart: 7 -> 9, of which waited for: 6 -> 4; matrix products, arithmetic and copies ran while one was open for 12% -> 9% of each run, Pallas kernels for 0% -> 0%
where the time goes in v1:
time: 166 us; the launch traced here: 165 us
  waiting for transfers between devices  103 us (62%)
  matrix products  21.8 us (13%)
  starting transfers between devices  20 us (12%)
  between operations  13.7 us (8%)
  local copies, waits for them, and re-layouts  4.04 us (2%)
  other arithmetic  3.09 us (2%)
    all_gather x1, waiting for transfers between devices, gathered_projection(): own = lax.all_gather(block, 'expert', axis_index_groups=groups)  46.8 us
    all_to_all x1, waiting for transfers between devices, shards(): lax.all_to_all(served, 'expert', split_axis=0, concat_axis=0, tiled=True)  24.5 us
    all_to_all x1, waiting for transfers between devices, shards(): lax.all_to_all(packed, 'expert', split_axis=0, concat_axis=0, tiled=True)  24 us
    dot_general x2, matrix products, half_expert(): jnp.dot(hidden, down_rows, preferred_element_type=jnp.float32)  8.7 us
    ppermute x1, waiting for transfers between devices, from_behind(): return lax.ppermute(block, axis, route)  6.93 us
    all_to_all x1, starting transfers between devices, shards(): lax.all_to_all(outgoing, 'expert', split_axis=0, concat_axis=0, tiled=True)  6.74 us
    dot_general x2, matrix products, half_expert(): gate_act = jnp.dot(rows, gate_cols, preferred_element_type=jnp.float32)  5.83 us
    all_to_all x1, starting transfers between devices, shards(): lax.all_to_all(served, 'expert', split_axis=0, concat_axis=0, tiled=True)  5.1 us
  transfers between devices with their start and end apart: 9, of which 4 were waited for; matrix products, arithmetic and copies ran while one was open for 9% of the time, Pallas kernels for 0%

profile of v1, /device:TPU:9, one launch (start us, length us, event | category | flops | bytes accessed | tf_op | source)
XLA Modules:
  0.0 165.4 jit_solution(10665029326135672277)
XLA Ops:
  6.5 0.8 and_select_fusion.3
  7.3 0.7 slice_bitcast_fusion.4
  8.4 1.6 fusion.2
  10.1 6.7 %all-to-all-start = ((bf16[16,8,5120]{2,1,0:T(8,128)(2,1)}), bf16[16,8,5120]{2,1,0:T(8,128)(2,1)S(1)}, u32[]{:S(2)}, u32[]{:S(2)}) async-start(bf16[16,8,5120]{2,1,0:T(8,128)(2,1)} %fusion.2), calls=%async_computation | async-start | bytes 2621440 | tf_op jit(solution)/shard_map/all_to_all | solution.py:121
  16.8 0.7 all-gather.2.cloned.1.call-update
  19.0 46.8 %all-gather.2.cloned.1.call-done = bf16[8,64,1024]{2,1,0:T(8,128)(2,1)} async-done(((bf16[1,64,1024]{2,1,0:T(8,128)(2,1)}), bf16[8,64,1024]{2,1,0:T(8,128)(2,1)}) %all-gather.2.cloned.1.call-update) | async-done | bytes 1048592 | tf_op jit(solution)/shard_map/all_gather | solution.py:94
  65.8 1.4 collective-permute-start
  67.2 0.5 fusion
  67.7 1.1 copy-done.1
  69.0 0.6 fusion.65
  70.0 1.2 multiply_convert_fusion.3
  71.8 1.7 %multiply_reduce_fusion = (f32[128]{0:T(128)S(1)}, f32[128,1024]{1,0:T(8,128)S(1)}) fusion(f32[128,1024]{1,0:T(8,128)S(1)} %fusion.72, bf16[128,512]{0,1:T(8,128)(2,1)S(1)} %bitcast.104, bf16[512,1024]{1,0:T(8,128)(2,1)} %bitcast.14, bf16[128,5120]{1,0:T(8,128)(2,1)} %copy-done.1), kind=kOutput, calls=%fused_computation.36 | convolution fusion | flops 135135104 | bytes 2490880 | tf_op jit(solution)/shard_map/dot_general | solution.py:139
  73.5 1.5 fusion.39
  75.0 4.6 %all-to-all-start.1 = ((bf16[16,32,1024]{2,1,0:T(8,128)(2,1)}), bf16[16,32,1024]{2,1,0:T(8,128)(2,1)S(1)}, u32[]{:S(2)}, u32[]{:S(2)}) async-start(bf16[16,32,1024]{2,1,0:T(8,128)(2,1)} %bitcast.16), calls=%async_computation.1 | async-start | bytes 2097152 | tf_op jit(solution)/shard_map/all_to_all | solution.py:156
  80.5 24.0 %all-to-all-done.1 = bf16[16,32,1024]{2,1,0:T(8,128)(2,1)S(1)} async-done(((bf16[16,32,1024]{2,1,0:T(8,128)(2,1)}), bf16[16,32,1024]{2,1,0:T(8,128)(2,1)S(1)}, u32[]{:S(2)}, u32[]{:S(2)}) %all-to-all-start.1) | async-done | bytes 1048608 | tf_op jit(solution)/shard_map/all_to_all | solution.py:156
  104.5 2.9 %fusion.57 = f32[512,512]{1,0:T(8,128)} fusion(bf16[512,1024]{1,0:T(8,128)(2,1)S(1)} %bitcast.97, bf16[1,1024,512]{2,1,0:T(8,128)(2,1)} %param.17), kind=kOutput, calls=%fused_computation.121 | convolution fusion | flops 536870912 | bytes 3145728 | tf_op jit(solution)/shard_map/dot_general | solution.py:85
  107.4 2.9 %fusion.73 = f32[512,512]{1,0:T(8,128)} fusion(bf16[512,1024]{1,0:T(8,128)(2,1)S(1)} %bitcast.98, bf16[1024,512]{1,0:T(8,128)(2,1)} %collective-permute-done.1), kind=kOutput, calls=%fused_computation.132 | convolution fusion | flops 536870912 | bytes 3145728 | tf_op jit(solution)/shard_map/dot_general | solution.py:85
  110.3 4.2 %convolution_convert_fusion.1 = bf16[512,1024]{1,0:T(8,128)(2,1)} fusion(bf16[512,1024]{1,0:T(8,128)(2,1)S(1)} %bitcast.99, f32[512,512]{1,0:T(8,128)} %fusion.57, bf16[1,512,1024]{2,1,0:T(8,128)(2,1)} %param.19, bf16[1,1024,512]{2,1,0:T(8,128)(2,1)} %param.18), kind=kOutput, calls=%fused_computation.2 | convolution fusion | flops 1075838976 | bytes 5242880 | tf_op jit(solution)/shard_map/dot_general | solution.py:88
  114.5 4.5 %add_convert_fusion = bf16[512,1024]{1,0:T(8,128)(2,1)} fusion(bf16[512,1024]{1,0:T(8,128)(2,1)} %convolution_convert_fusion.1, bf16[512,1024]{1,0:T(8,128)(2,1)} %collective-permute-done.3, f32[512,512]{1,0:T(8,128)} %fusion.73, bf16[512,1024]{1,0:T(8,128)(2,1)S(1)} %bitcast.100, bf16[1024,512]{1,0:T(8,128)(2,1)} %collective-permute-done.2), kind=kOutput, calls=%fused_computation | convolution fusion | flops 1077936128 | bytes 6291456 | tf_op jit(solution)/shard_map/dot_general | solution.py:88
  119.0 5.1 %all-to-all-start.2 = ((bf16[16,32,1024]{2,1,0:T(8,128)(2,1)}), bf16[16,32,1024]{2,1,0:T(8,128)(2,1)S(1)}, u32[]{:S(2)}, u32[]{:S(2)}) async-start(bf16[16,32,1024]{2,1,0:T(8,128)(2,1)} %bitcast.101), calls=%async_computation.2 | async-start | bytes 2097152 | tf_op jit(solution)/shard_map/all_to_all | solution.py:160
  124.5 24.5 %all-to-all-done.2 = bf16[16,32,1024]{2,1,0:T(8,128)(2,1)S(1)} async-done(((bf16[16,32,1024]{2,1,0:T(8,128)(2,1)}), bf16[16,32,1024]{2,1,0:T(8,128)(2,1)S(1)}, u32[]{:S(2)}, u32[]{:S(2)}) %all-to-all-start.2) | async-done | bytes 1048608 | tf_op jit(solution)/shard_map/all_to_all | solution.py:160
  149.7 1.3 collective-permute-start.4
  150.9 6.9 %collective-permute-done.4 = bf16[1,128,1024]{2,1,0:T(8,128)(2,1)S(1)} collective-permute-done((bf16[1,128,1024]{2,1,0:T(8,128)(2,1)S(1)}, bf16[1,128,1024]{2,1,0:T(8,128)(2,1)S(1)}, u32[]{:S(2)}, u32[]{:S(2)}) %collective-permute-start.4) | collective-permute-done | bytes 262176 | tf_op jit(solution)/shard_map/ppermute | solution.py:16
  157.9 0.7 copy.68
  (65 shorter events, 4.9 us)
Async XLA Ops:
  6.5 1.9 %copy-start = (bf16[1,128,5120]{2,1,0:T(8,128)(2,1)S(1)}, bf16[1,128,5120]{2,1,0:T(8,128)(2,1)}, u32[]{:S(2)}) copy-start(bf16[1,128,5120]{2,1,0:T(8,128)(2,1)} %param.10) | copy-start | bytes 3932164
  10.1 7.7 %copy-start.6 = (s32[1,1,4]{2,1,0:T(1,128)S(1)}, s32[1,1,4]{2,1,0:T(1,128)}, u32[]{:S(2)}) copy-start(s32[1,1,4]{2,1,0:T(1,128)} %param.12) | copy-start | bytes 52
  10.1 7.9 %copy-start.5 = (s32[1,1,4]{2,1,0:T(1,128)S(1)}, s32[1,1,4]{2,1,0:T(1,128)}, u32[]{:S(2)}) copy-start(s32[1,1,4]{2,1,0:T(1,128)} %param.13) | copy-start | bytes 52
  10.1 8.0 %copy-start.4 = (s32[1,128,2]{1,2,0:T(2,128)S(1)}, s32[1,128,2]{1,2,0:T(2,128)}, u32[]{:S(2)}) copy-start(s32[1,128,2]{1,2,0:T(2,128)} %param.14) | copy-start | bytes 3076
  10.1 57.1 %all-to-all-start = ((bf16[16,8,5120]{2,1,0:T(8,128)(2,1)}), bf16[16,8,5120]{2,1,0:T(8,128)(2,1)S(1)}, u32[]{:S(2)}, u32[]{:S(2)}) async-start(bf16[16,8,5120]{2,1,0:T(8,128)(2,1)} %fusion.2), calls=%async_computation | async-start | bytes 2621440 | tf_op jit(solution)/shard_map/all_to_all | solution.py:121
  16.8 49.0 %all-gather.2.cloned.1.call-start = ((), (), s32[]{:S(2)}) async-start(), calls=%async_computation.3 | async-start | bytes 1179648 | tf_op jit(solution)/shard_map/all_gather | solution.py:94
  65.8 5.9 %collective-permute-start = (bf16[8,64,1024]{2,1,0:T(8,128)(2,1)}, bf16[8,64,1024]{2,1,0:T(8,128)(2,1)}, u32[]{:S(2)}, u32[]{:S(2)}) collective-permute-start(bf16[8,64,1024]{2,1,0:T(8,128)(2,1)} %all-gather.2.cloned.1.call-done), channel_id=1, source_target_pairs={{0,1},{1,0},{2,3},{3,2},{4,5},{5,4},{6,7},{7,6},{8,9},{9,8},{10,11... | collective-permute-start | bytes 3145736 | tf_op jit(solution)/shard_map/ppermute | solution.py:10
  67.7 1.1 copy-start.1
  69.8 1.6 copy-start.2
  75.0 29.5 %all-to-all-start.1 = ((bf16[16,32,1024]{2,1,0:T(8,128)(2,1)}), bf16[16,32,1024]{2,1,0:T(8,128)(2,1)S(1)}, u32[]{:S(2)}, u32[]{:S(2)}) async-start(bf16[16,32,1024]{2,1,0:T(8,128)(2,1)} %bitcast.16), calls=%async_computation.1 | async-start | bytes 2097152 | tf_op jit(solution)/shard_map/all_to_all | solution.py:156
  79.6 27.8 %collective-permute-start.1 = (bf16[1024,512]{1,0:T(8,128)(2,1)}, bf16[1024,512]{1,0:T(8,128)(2,1)}, u32[]{:S(2)}, u32[]{:S(2)}) collective-permute-start(bf16[1024,512]{1,0:T(8,128)(2,1)} %bitcast.107), channel_id=1, source_target_pairs={{0,1},{1,0},{2,3},{3,2},{4,5},{5,4},{6,7},{7,6},{8,9},{9,8},{10,11... | collective-permute-start | bytes 3145736 | tf_op jit(solution)/shard_map/ppermute | solution.py:10
  80.0 34.5 %collective-permute-start.2 = (bf16[1024,512]{1,0:T(8,128)(2,1)}, bf16[1024,512]{1,0:T(8,128)(2,1)}, u32[]{:S(2)}, u32[]{:S(2)}) collective-permute-start(bf16[1024,512]{1,0:T(8,128)(2,1)} %bitcast.108), channel_id=1, source_target_pairs={{0,1},{1,0},{2,3},{3,2},{4,5},{5,4},{6,7},{7,6},{8,9},{9,8},{10,11... | collective-permute-start | bytes 3145736 | tf_op jit(solution)/shard_map/ppermute | solution.py:10
  80.1 34.4 %collective-permute-start.3 = (bf16[512,1024]{1,0:T(8,128)(2,1)}, bf16[512,1024]{1,0:T(8,128)(2,1)}, u32[]{:S(2)}, u32[]{:S(2)}) collective-permute-start(bf16[512,1024]{1,0:T(8,128)(2,1)} %bitcast.109), channel_id=1, source_target_pairs={{0,1},{1,0},{2,3},{3,2},{4,5},{5,4},{6,7},{7,6},{8,9},{9,8},{10,11... | collective-permute-start | bytes 3145736 | tf_op jit(solution)/shard_map/ppermute | solution.py:10
  119.0 5.2 %copy-start.3 = (bf16[1,1024,8]{1,2,0:T(8,128)(2,1)S(1)}, bf16[1,1024,8]{1,2,0:T(8,128)(2,1)}, u32[]{:S(2)}) copy-start(bf16[1,1024,8]{1,2,0:T(8,128)(2,1)} %param.16) | copy-start | bytes 49156
  119.0 29.9 %all-to-all-start.2 = ((bf16[16,32,1024]{2,1,0:T(8,128)(2,1)}), bf16[16,32,1024]{2,1,0:T(8,128)(2,1)S(1)}, u32[]{:S(2)}, u32[]{:S(2)}) async-start(bf16[16,32,1024]{2,1,0:T(8,128)(2,1)} %bitcast.101), calls=%async_computation.2 | async-start | bytes 2097152 | tf_op jit(solution)/shard_map/all_to_all | solution.py:160
  149.7 8.2 %collective-permute-start.4 = (bf16[1,128,1024]{2,1,0:T(8,128)(2,1)S(1)}, bf16[1,128,1024]{2,1,0:T(8,128)(2,1)S(1)}, u32[]{:S(2)}, u32[]{:S(2)}) collective-permute-start(bf16[1,128,1024]{2,1,0:T(8,128)(2,1)S(1)} %fusion.11), channel_id=1, source_target_pairs={{16,0},{0,16},{17,1},{1,17},{18,2},{2,18},{19,3},{3,19},{20,4},{4,... | collective-permute-start | bytes 786440 | tf_op jit(solution)/shard_map/ppermute | solution.py:16
Sparse Core Ops, SparseCore 0:
  19.8 46.0 all-gather.1

commit v2 on v1

--- a/solution.py
+++ b/solution.py
@@ -1,6 +1,8 @@
 import jax
 import jax.numpy as jnp
 from jax import lax
+from jax.experimental import pallas as pl
+from jax.experimental.pallas import tpu as pltpu
 from jax.sharding import PartitionSpec as P
 
 HEADS = 8
@@ -81,24 +83,70 @@
     return jnp.broadcast_to(pages[:, None], (pages.shape[0], page_rows)).reshape(-1)
 
 
-def half_expert(rows, gate_cols, up_cols, down_rows):
-    gate_act = jnp.dot(rows, gate_cols, preferred_element_type=jnp.float32)
-    up_act = jnp.dot(rows, up_cols, preferred_element_type=jnp.float32)
-    hidden = (jax.nn.silu(gate_act) * up_act).astype(jnp.bfloat16)
-    return jnp.dot(hidden, down_rows, preferred_element_type=jnp.float32).astype(jnp.bfloat16)
+def expert_kernel(rows_ref, gate0, up0, down0, gate1, up1, down1, out_ref, hidden_ref):
+    units = gate0.shape[1]
+    tile = 256 if units % 256 == 0 else units
+    for half, (gate_ref, up_ref, down_ref) in enumerate(((gate0, up0, down0), (gate1, up1, down1))):
+        for first in range(0, units, tile):
+            span = slice(first, first + tile)
+            gate_act = jnp.dot(
+                rows_ref[...], gate_ref[:, span], preferred_element_type=jnp.float32
+            )
+            up_act = jnp.dot(rows_ref[...], up_ref[:, span], preferred_element_type=jnp.float32)
+            hidden_ref[:, span] = (jax.nn.silu(gate_act) * up_act).astype(jnp.bfloat16)
+        for first in range(0, out_ref.shape[1], tile):
+            span = slice(first, first + tile)
+            part = jnp.dot(
+                hidden_ref[...], down_ref[:, span], preferred_element_type=jnp.float32
+            ).astype(jnp.bfloat16)
+            if half == 0:
+                out_ref[:, span] = part
+            else:
+                earlier = out_ref[:, span].astype(jnp.float32)
+                out_ref[:, span] = (earlier + part.astype(jnp.float32)).astype(jnp.bfloat16)
+
+
+def whole_expert(rows, *weights):
+    count, width = rows.shape
+    units = weights[0].shape[1]
+    return pl.pallas_call(
+        expert_kernel,
+        out_shape=jax.ShapeDtypeStruct((count, width), jnp.bfloat16),
+        in_specs=[pl.BlockSpec(memory_space=pltpu.VMEM)] * 7,
+        out_specs=pl.BlockSpec(memory_space=pltpu.VMEM),
+        scratch_shapes=[pltpu.VMEM((count, units), jnp.bfloat16)],
+        compiler_params=pltpu.CompilerParams(vmem_limit_bytes=32 * 1024 * 1024),
+        cost_estimate=pl.CostEstimate(
+            flops=12 * count * width * units,
+            bytes_accessed=12 * width * units + 4 * count * width,
+            transcendentals=2 * count * units,
+        ),
+        name="expert_pair",
+    )(rows, *weights)
 
 
 def gathered_projection(block):
     devices = lax.axis_size("expert")
-    groups = [list(range(first, devices, 2)) for first in range(2)]
-    own = lax.all_gather(block, "expert", axis_index_groups=groups)
-    return own, swapped(own, "expert", 0)
+    me = lax.axis_index("expert")
+    rows = block.shape[0]
+    line = [block] + [from_behind(block, "expert", 4 * k) for k in range(1, devices // 4)]
+    line = jnp.concatenate(line, axis=0)
+    plane = jnp.concatenate([line, swapped(line, "expert", 1)], axis=0)
+    other = swapped(plane, "expert", 0)
+    slot = jnp.arange(devices * rows, dtype=jnp.int32)
+    turn, inner = slot // rows, slot % rows
+    steps = turn % (devices // 4)
+    side = (turn // (devices // 4)) % 2
+    core = turn // (devices // 2)
+    line_at = (me // 4 - steps + devices // 4) % (devices // 4)
+    side_at = (me // 2 + side) % 2
+    core_at = (me + core) % 2
+    return plane, other, (line_at * 4 + side_at * 2 + core_at) * rows + inner
 
 
 def shards(histories, page_map, user_pages, tails, routes, out_proj, router, w_gate, w_up, w_down):
     devices = lax.axis_size("expert")
-    parity = lax.axis_index("expert") % 2
-    own_proj, other_proj = gathered_projection(out_proj[0])
+    own_proj, other_proj, proj_row = gathered_projection(out_proj[0])
     other_gate = swapped(w_gate[0], "expert", 0)
     other_up = swapped(w_up[0], "expert", 0)
     other_down = swapped(w_down[0], "expert", 0)
@@ -128,16 +176,14 @@
     taking = (comes_from[:, None] == wire_row[None, :]).astype(jnp.bfloat16)
     balanced = jnp.dot(taking, arrived)
     mixed_in = attend(balanced, user_pages[0, 0], tails[0, 0], page_rows)
-    is_odd = parity == 1
-    even_odd = mixed_in.reshape(row_count, devices // 2, 2, out_proj.shape[1])
-    even = even_odd[:, :, 0].reshape(row_count, -1)
-    odd = even_odd[:, :, 1].reshape(row_count, -1)
-    own_mixed = jnp.where(is_odd, odd, even)
-    other_mixed = jnp.where(is_odd, even, odd)
+    columns = jnp.arange(model_width, dtype=jnp.int32)
+    ordering_of = (columns[:, None] == proj_row[None, :]).astype(jnp.bfloat16)
+    ordered = jnp.dot(mixed_in, ordering_of)
+    own_mixed, other_mixed = ordered[:, : model_width // 2], ordered[:, model_width // 2 :]
     projected = jnp.dot(
-        own_mixed, own_proj.reshape(-1, model_width), preferred_element_type=jnp.float32
+        own_mixed, own_proj, preferred_element_type=jnp.float32
     ) + jnp.dot(
-        other_mixed, other_proj.reshape(-1, model_width), preferred_element_type=jnp.float32
+        other_mixed, other_proj, preferred_element_type=jnp.float32
     )
     resid = (balanced[:, 4 * model_width :].astype(jnp.float32) + projected).astype(jnp.bfloat16)
     resid_wide = resid.astype(jnp.float32)
@@ -154,9 +200,9 @@
     ).astype(jnp.bfloat16)
     packed = jnp.dot(packing, normed)
     own_rows = lax.all_to_all(packed, "expert", split_axis=0, concat_axis=0, tiled=True)
-    own_part = half_expert(own_rows, w_gate[0], w_up[0], w_down[0])
-    other_part = half_expert(own_rows, other_gate, other_up, other_down)
-    served = (own_part.astype(jnp.float32) + other_part.astype(jnp.float32)).astype(jnp.bfloat16)
+    served = whole_expert(
+        own_rows, w_gate[0], w_up[0], w_down[0], other_gate, other_up, other_down
+    )
     came_back = lax.all_to_all(served, "expert", split_axis=0, concat_axis=0, tiled=True)
     mixture = jnp.zeros_like(resid_wide)
     for k in range(slots.shape[1]):

time: 166 us -> 135 us (0.81)
  waiting for transfers between devices: 103 us -> 73.8 us
  local copies, waits for them, and re-layouts: 4.04 us -> 18.8 us
  between operations: 13.7 us -> 0.36 us
  matrix products: 21.8 us -> 10.1 us
  starting transfers between devices: 20 us -> 24.7 us
  Pallas kernels: 0 us -> 4.41 us
    all_gather x1 -> x0, waiting for transfers between devices: 46.8 us -> none  [gathered_projection(): own = lax.all_gather(block, 'expert', axis_index_groups=groups)]
    ppermute x4 -> x5, waiting for transfers between devices: 0.01 us -> 21.7 us  [swapped(): lax.ppermute(shard, axis, [(i, i ^ 1 << apart) for i in range(lax.axis_si...]
    unnamed x17 -> x47, local copies, waits for them, and re-layouts: 1.95 us -> 16 us
    dot_general x6 -> x3, matrix products: 16.6 us -> 4.91 us  [the longest x1 1.95 us: shards(): ordered = jnp.dot(mixed_in, ordering_of)]
    all_to_all x1, waiting for transfers between devices: 24 us -> 17.9 us  [shards(): lax.all_to_all(packed, 'expert', split_axis=0, concat_axis=0, tiled=True)]
    pallas_call x0 -> x1, Pallas kernels: none -> 4.41 us  [whole_expert(): pl.pallas_call(expert_kernel, out_shape=jax.ShapeDtypeStruct((count, widt...]
    ppermute x1 -> x4, starting transfers between devices: 1.26 us -> 5.06 us  [from_behind(): return lax.ppermute(block, axis, route)]
    all_to_all x1, waiting for transfers between devices: 0.01 us -> 2.82 us  [shards(): lax.all_to_all(outgoing, 'expert', split_axis=0, concat_axis=0, tiled=True)]
  transfers between devices with their start and end apart: 9 -> 12, of which waited for: 4 -> 8; matrix products, arithmetic and copies ran while one was open for 9% -> 10% of each run, Pallas kernels for 0% -> 0%
where the time goes in v2:
time: 135 us; the launch traced here: 134 us
  waiting for transfers between devices  73.8 us (55%)
  starting transfers between devices  24.7 us (18%)
  local copies, waits for them, and re-layouts  18.8 us (14%)
  matrix products  10.1 us (7%)
  Pallas kernels  4.41 us (3%)
  other arithmetic  1.87 us (1%)
    all_to_all x1, waiting for transfers between devices, shards(): lax.all_to_all(served, 'expert', split_axis=0, concat_axis=0, tiled=True)  24.4 us
    ppermute x5, waiting for transfers between devices, swapped(): lax.ppermute(shard, axis, [(i, i ^ 1 << apart) for i in range(lax.axis_si...  21.7 us
    all_to_all x1, waiting for transfers between devices, shards(): lax.all_to_all(packed, 'expert', split_axis=0, concat_axis=0, tiled=True)  17.9 us
    unnamed x47, local copies, waits for them, and re-layouts  16 us
    ppermute x4, waiting for transfers between devices, from_behind(): return lax.ppermute(block, axis, route)  6.91 us
    all_to_all x1, starting transfers between devices, shards(): lax.all_to_all(outgoing, 'expert', split_axis=0, concat_axis=0, tiled=True)  6.16 us
    all_to_all x1, starting transfers between devices, shards(): lax.all_to_all(packed, 'expert', split_axis=0, concat_axis=0, tiled=True)  5.38 us
    all_to_all x1, starting transfers between devices, shards(): lax.all_to_all(served, 'expert', split_axis=0, concat_axis=0, tiled=True)  5.1 us
  transfers between devices with their start and end apart: 12, of which 8 were waited for; matrix products, arithmetic and copies ran while one was open for 10% of the time, Pallas kernels for 0%

profile of v2, /device:TPU:9, one launch (start us, length us, event | category | flops | bytes accessed | tf_op | source)
XLA Modules:
  0.0 134.0 jit_solution(2488208201820093196)
XLA Ops:
  0.0 1.3 collective-permute-start
  2.4 1.4 %collective-permute-start.2 = (bf16[64,1024]{1,0:T(8,128)(2,1)}, bf16[64,1024]{1,0:T(8,128)(2,1)S(1)}, u32[]{:S(2)}, u32[]{:S(2)}) collective-permute-start(bf16[64,1024]{1,0:T(8,128)(2,1)} %bitcast.87), channel_id=1, source_target_pairs={{4,0},{5,1},{6,2},{7,3},{8,4},{9,5},{10,6},{11,7},{12,8},{13,9},{1... | collective-permute-start | bytes 393224 | tf_op jit(solution)/shard_map/ppermute | solution.py:18
  5.6 1.6 %fusion.4 = bf16[16,8,5120]{2,1,0:T(8,128)(2,1)} fusion(bf16[1,128,5120]{2,1,0:T(8,128)(2,1)S(1)} %copy-done, s32[128]{0:T(128)S(1)} %fusion.78, s32[16,8]{1,0:T(8,128)S(1)} %multiply_add_fusion.1), kind=kOutput, calls=%fused_computation.5 | convolution fusion | flops 167788544 | bytes 2622464 | tf_op jit(solution)/shard_map/dot_general | solution.py:168
  7.3 6.2 %all-to-all-start = ((bf16[16,8,5120]{2,1,0:T(8,128)(2,1)}), bf16[16,8,5120]{2,1,0:T(8,128)(2,1)S(1)}, u32[]{:S(2)}, u32[]{:S(2)}) async-start(bf16[16,8,5120]{2,1,0:T(8,128)(2,1)} %fusion.4), calls=%async_computation | async-start | bytes 2621440 | tf_op jit(solution)/shard_map/all_to_all | solution.py:169
  16.3 1.3 collective-permute-start.3
  18.9 1.6 %constant_dynamic-update-slice_fusion.1 = bf16[512,1024]{1,0:T(8,128)(2,1)} fusion(bf16[512,1024]{1,0:T(8,128)(2,1)} %constant_dynamic-update-slice_fusion.2, bf16[64,1024]{1,0:T(8,128)(2,1)} %copy-done.15), kind=kLoop, calls=%fused_computation.76 | loop fusion | bytes 262144
  20.4 18.7 %collective-permute-done.3 = bf16[256,1024]{1,0:T(8,128)(2,1)S(1)} collective-permute-done((bf16[256,1024]{1,0:T(8,128)(2,1)S(1)}, bf16[256,1024]{1,0:T(8,128)(2,1)S(1)}, u32[]{:S(2)}, u32[]{:S(2)}) %collective-permute-start.3) | collective-permute-done | bytes 524320 | tf_op jit(solution)/shard_map/ppermute | solution.py:12
  40.8 2.8 %all-to-all-done = bf16[16,8,5120]{2,1,0:T(8,128)(2,1)S(1)} async-done(((bf16[16,8,5120]{2,1,0:T(8,128)(2,1)}), bf16[16,8,5120]{2,1,0:T(8,128)(2,1)S(1)}, u32[]{:S(2)}, u32[]{:S(2)}) %all-to-all-start) | async-done | bytes 1310752 | tf_op jit(solution)/shard_map/all_to_all | solution.py:169
  46.4 1.9 %fusion = bf16[128,1024]{1,0:T(8,128)(2,1)S(1)} fusion(s32[1024]{0:T(1024)S(1)} %fusion.65, f32[128,1024]{1,0:T(8,128)S(1)} %copy.39, bf16[128,5120]{1,0:T(8,128)(2,1)} %copy-done.12, f32[128]{0:T(128)S(1)} %add_rsqrt_fusion.1, f32[128]{0:T(128)S(1)} %broadcast_multiply_fusion), kind=kOutput, calls=%fused_computation.1 | convolution fusion | flops 270139392 | bytes 1053696 | tf_op jit(solution)/shard_map/dot_general | solution.py:181
  48.4 1.6 %fusion.39 = f32[128,1024]{1,0:T(8,128)S(1)} fusion(bf16[512,1024]{1,0:T(8,128)(2,1)} %collective-permute-done.4, bf16[128,1024]{1,0:T(8,128)(2,1)S(1)} %fusion), kind=kOutput, calls=%fused_computation.54 | convolution fusion | flops 134217728 | bytes 1703936 | tf_op jit(solution)/shard_map/dot_general | solution.py:185
  50.0 1.4 %multiply_reduce_fusion = (f32[128]{0:T(128)S(1)}, f32[128,1024]{1,0:T(8,128)S(1)}) fusion(f32[128,1024]{1,0:T(8,128)S(1)} %fusion.39, bf16[512,1024]{1,0:T(8,128)(2,1)S(1)} %copy-done.13, bf16[128,1024]{1,0:T(8,128)(2,1)S(1)} %fusion, bf16[128,5120]{1,0:T(8,128)(2,1)} %copy-done.12), kind=kOutput, calls=%fused_computation.27 | convolution fusion | flops 135135104 | bytes 2490880 | tf_op jit(solution)/shard_map/dot_general | solution.py:183
  52.2 1.5 %fusion.36 = bf16[512,1024]{1,0:T(8,128)(2,1)} fusion(s32[128]{0:T(128)S(1)} %get-tuple-element.6, s32[128]{0:T(128)S(1)} %get-tuple-element.5, f32[128,1024]{1,0:T(8,128)S(1)} %get-tuple-element.21, f32[128]{0:T(128)S(1)} %add_rsqrt_fusion), kind=kOutput, calls=%fused_computation.52 | convolution fusion | flops 134676480 | bytes 1574400 | tf_op jit(solution)/shard_map/dot_general | solution.py:201
  53.7 5.4 %all-to-all-start.1 = ((bf16[16,32,1024]{2,1,0:T(8,128)(2,1)}), bf16[16,32,1024]{2,1,0:T(8,128)(2,1)S(1)}, u32[]{:S(2)}, u32[]{:S(2)}) async-start(bf16[16,32,1024]{2,1,0:T(8,128)(2,1)} %bitcast.82), calls=%async_computation.1 | async-start | bytes 2097152 | tf_op jit(solution)/shard_map/all_to_all | solution.py:202
  60.0 1.8 %collective-permute-done.5.gate1 = bf16[1024,512]{1,0:T(8,128)(2,1)S(1)} collective-permute-done((bf16[1024,512]{1,0:T(8,128)(2,1)S(1)}, bf16[1024,512]{1,0:T(8,128)(2,1)S(1)}, u32[]{:S(2)}, u32[]{:S(2)}) %collective-permute-start.5) | collective-permute-done | bytes 1048608 | tf_op jit(solution)/shard_map/ppermute | solution.py:12
  66.0 17.9 %all-to-all-done.1 = bf16[16,32,1024]{2,1,0:T(8,128)(2,1)S(1)} async-done(((bf16[16,32,1024]{2,1,0:T(8,128)(2,1)}), bf16[16,32,1024]{2,1,0:T(8,128)(2,1)S(1)}, u32[]{:S(2)}, u32[]{:S(2)}) %all-to-all-start.1) | async-done | bytes 1048608 | tf_op jit(solution)/shard_map/all_to_all | solution.py:202
  83.9 1.2 copy-done.2
  85.1 1.2 copy-done.3
  86.4 1.2 copy-done.5
  87.6 1.2 copy-done.7
  90.0 4.4 %expert_pair.1 = bf16[512,1024]{1,0:T(8,128)(2,1)} custom-call(bf16[512,1024]{1,0:T(8,128)(2,1)S(1)} %bitcast.73, bf16[1024,512]{1,0:T(8,128)(2,1)S(1)} %bitcast.75, bf16[1024,512]{1,0:T(8,128)(2,1)S(1)} %bitcast.77, bf16[512,1024]{1,0:T(8,128)(2,1)S(1)} %bitcast.79, bf16[1024,512]{1,0:T(8,128)(2,1)S(1)} %copy-done.5, bf16[1024,512]{1,0:T(8,128)(2,1)S(1)} %copy-done.7, ...), custom_call_target="tpu_custom_call" | custom-call | flops 3221225472 | bytes 8388608 | tf_op jit(solution)/shard_map/expert_pair/pallas_call | solution.py:112
  94.4 5.1 %all-to-all-start.2 = ((bf16[16,32,1024]{2,1,0:T(8,128)(2,1)}), bf16[16,32,1024]{2,1,0:T(8,128)(2,1)S(1)}, u32[]{:S(2)}, u32[]{:S(2)}) async-start(bf16[16,32,1024]{2,1,0:T(8,128)(2,1)} %bitcast.17), calls=%async_computation.2 | async-start | bytes 2097152 | tf_op jit(solution)/shard_map/all_to_all | solution.py:206
  99.9 24.4 %all-to-all-done.2 = bf16[16,32,1024]{2,1,0:T(8,128)(2,1)S(1)} async-done(((bf16[16,32,1024]{2,1,0:T(8,128)(2,1)}), bf16[16,32,1024]{2,1,0:T(8,128)(2,1)S(1)}, u32[]{:S(2)}, u32[]{:S(2)}) %all-to-all-start.2) | async-done | bytes 1048608 | tf_op jit(solution)/shard_map/all_to_all | solution.py:206
  125.1 1.3 collective-permute-start.8
  126.4 6.9 %collective-permute-done.8 = bf16[1,128,1024]{2,1,0:T(8,128)(2,1)S(1)} collective-permute-done((bf16[1,128,1024]{2,1,0:T(8,128)(2,1)S(1)}, bf16[1,128,1024]{2,1,0:T(8,128)(2,1)S(1)}, u32[]{:S(2)}, u32[]{:S(2)}) %collective-permute-start.8) | collective-permute-done | bytes 262176 | tf_op jit(solution)/shard_map/ppermute | solution.py:18
  (98 shorter events, 20.3 us)
Async XLA Ops:
  0.0 5.6 %copy-start = (bf16[1,128,5120]{2,1,0:T(8,128)(2,1)S(1)}, bf16[1,128,5120]{2,1,0:T(8,128)(2,1)}, u32[]{:S(2)}) copy-start(bf16[1,128,5120]{2,1,0:T(8,128)(2,1)} %param.10) | copy-start | bytes 3932164
  0.0 15.6 %collective-permute-start = (bf16[64,1024]{1,0:T(8,128)(2,1)}, bf16[64,1024]{1,0:T(8,128)(2,1)S(1)}, u32[]{:S(2)}, u32[]{:S(2)}) collective-permute-start(bf16[64,1024]{1,0:T(8,128)(2,1)} %bitcast.85), channel_id=1, source_target_pairs={{12,0},{13,1},{14,2},{15,3},{0,4},{1,5},{2,6},{3,7},{4,8},{5,9},{6... | collective-permute-start | bytes 393224 | tf_op jit(solution)/shard_map/ppermute | solution.py:18
  1.3 14.3 %collective-permute-start.1 = (bf16[64,1024]{1,0:T(8,128)(2,1)}, bf16[64,1024]{1,0:T(8,128)(2,1)S(1)}, u32[]{:S(2)}, u32[]{:S(2)}) collective-permute-start(bf16[64,1024]{1,0:T(8,128)(2,1)} %bitcast.86), channel_id=1, source_target_pairs={{8,0},{9,1},{10,2},{11,3},{12,4},{13,5},{14,6},{15,7},{0,8},{1,9},... | collective-permute-start | bytes 393224 | tf_op jit(solution)/shard_map/ppermute | solution.py:18
  2.4 13.2 %collective-permute-start.2 = (bf16[64,1024]{1,0:T(8,128)(2,1)}, bf16[64,1024]{1,0:T(8,128)(2,1)S(1)}, u32[]{:S(2)}, u32[]{:S(2)}) collective-permute-start(bf16[64,1024]{1,0:T(8,128)(2,1)} %bitcast.87), channel_id=1, source_target_pairs={{4,0},{5,1},{6,2},{7,3},{8,4},{9,5},{10,6},{11,7},{12,8},{13,9},{1... | collective-permute-start | bytes 393224 | tf_op jit(solution)/shard_map/ppermute | solution.py:18
  7.2 6.2 %copy-start.19 = (s32[1,1,4]{2,1,0:T(1,128)S(1)}, s32[1,1,4]{2,1,0:T(1,128)}, u32[]{:S(2)}) copy-start(s32[1,1,4]{2,1,0:T(1,128)} %param.12) | copy-start | bytes 52
  7.2 6.4 %copy-start.18 = (s32[1,1,4]{2,1,0:T(1,128)S(1)}, s32[1,1,4]{2,1,0:T(1,128)}, u32[]{:S(2)}) copy-start(s32[1,1,4]{2,1,0:T(1,128)} %param.13) | copy-start | bytes 52
  7.2 6.4 %copy-start.17 = (s32[1,128,2]{1,2,0:T(2,128)S(1)}, s32[1,128,2]{1,2,0:T(2,128)}, u32[]{:S(2)}) copy-start(s32[1,128,2]{1,2,0:T(2,128)} %param.14) | copy-start | bytes 3076
  7.3 7.3 %copy-start.14 = (bf16[1,64,1024]{2,1,0:T(8,128)(2,1)S(1)}, bf16[1,64,1024]{2,1,0:T(8,128)(2,1)}, u32[]{:S(2)}) copy-start(bf16[1,64,1024]{2,1,0:T(8,128)(2,1)} %param.15) | copy-start | bytes 393220
  7.3 36.4 %all-to-all-start = ((bf16[16,8,5120]{2,1,0:T(8,128)(2,1)}), bf16[16,8,5120]{2,1,0:T(8,128)(2,1)S(1)}, u32[]{:S(2)}, u32[]{:S(2)}) async-start(bf16[16,8,5120]{2,1,0:T(8,128)(2,1)} %fusion.4), calls=%async_computation | async-start | bytes 2621440 | tf_op jit(solution)/shard_map/all_to_all | solution.py:169
  16.3 22.9 %collective-permute-start.3 = (bf16[256,1024]{1,0:T(8,128)(2,1)S(1)}, bf16[256,1024]{1,0:T(8,128)(2,1)S(1)}, u32[]{:S(2)}, u32[]{:S(2)}) collective-permute-start(bf16[256,1024]{1,0:T(8,128)(2,1)S(1)} %pad_maximum_fusion), channel_id=1, source_target_pairs={{0,2},{1,3},{2,0},{3,1},{4,6},{5,7},{6,4},{7,5},{8,10},{9,11},{10,... | collective-permute-start | bytes 1572872 | tf_op jit(solution)/shard_map/ppermute | solution.py:12
  40.0 8.4 %collective-permute-start.4 = (bf16[512,1024]{1,0:T(8,128)(2,1)}, bf16[512,1024]{1,0:T(8,128)(2,1)}, u32[]{:S(2)}, u32[]{:S(2)}) collective-permute-start(bf16[512,1024]{1,0:T(8,128)(2,1)} %constant_dynamic-update-slice_fusion), channel_id=1, source_target_pairs={{0,1},{1,0},{2,3},{3,2},{4,5},{5,4},{6,7},{7,6},{8,9},{9,8},{10,11... | collective-permute-start | bytes 3145736 | tf_op jit(solution)/shard_map/ppermute | solution.py:12
  48.4 1.6 %copy-start.13 = (bf16[512,1024]{1,0:T(8,128)(2,1)S(1)}, bf16[512,1024]{1,0:T(8,128)(2,1)}, u32[]{:S(2)}) copy-start(bf16[512,1024]{1,0:T(8,128)(2,1)} %constant_dynamic-update-slice_fusion) | copy-start | bytes 3145732
  53.7 5.4 %copy-start.1 = (bf16[1,1024,512]{2,1,0:T(8,128)(2,1)S(1)}, bf16[1,1024,512]{2,1,0:T(8,128)(2,1)}, u32[]{:S(2)}) copy-start(bf16[1,1024,512]{2,1,0:T(8,128)(2,1)} %param.17) | copy-start | bytes 3145732
  53.7 30.2 %all-to-all-start.1 = ((bf16[16,32,1024]{2,1,0:T(8,128)(2,1)}), bf16[16,32,1024]{2,1,0:T(8,128)(2,1)S(1)}, u32[]{:S(2)}, u32[]{:S(2)}) async-start(bf16[16,32,1024]{2,1,0:T(8,128)(2,1)} %bitcast.82), calls=%async_computation.1 | async-start | bytes 2097152 | tf_op jit(solution)/shard_map/all_to_all | solution.py:202
  59.1 2.7 %collective-permute-start.5 = (bf16[1024,512]{1,0:T(8,128)(2,1)S(1)}, bf16[1024,512]{1,0:T(8,128)(2,1)S(1)}, u32[]{:S(2)}, u32[]{:S(2)}) collective-permute-start(bf16[1024,512]{1,0:T(8,128)(2,1)S(1)} %bitcast.74), channel_id=1, source_target_pairs={{0,1},{1,0},{2,3},{3,2},{4,5},{5,4},{6,7},{7,6},{8,9},{9,8},{10,11... | collective-permute-start | bytes 3145736 | tf_op jit(solution)/shard_map/ppermute | solution.py:12
  59.5 4.0 %collective-permute-start.6 = (bf16[1024,512]{1,0:T(8,128)(2,1)}, bf16[1024,512]{1,0:T(8,128)(2,1)S(1)}, u32[]{:S(2)}, u32[]{:S(2)}) collective-permute-start(bf16[1024,512]{1,0:T(8,128)(2,1)} %bitcast.76), channel_id=1, source_target_pairs={{0,1},{1,0},{2,3},{3,2},{4,5},{5,4},{6,7},{7,6},{8,9},{9,8},{10,11... | collective-permute-start | bytes 3145736 | tf_op jit(solution)/shard_map/ppermute | solution.py:12
  59.6 5.4 %collective-permute-start.7 = (bf16[512,1024]{1,0:T(8,128)(2,1)}, bf16[512,1024]{1,0:T(8,128)(2,1)S(1)}, u32[]{:S(2)}, u32[]{:S(2)}) collective-permute-start(bf16[512,1024]{1,0:T(8,128)(2,1)} %bitcast.78), channel_id=1, source_target_pairs={{0,1},{1,0},{2,3},{3,2},{4,5},{5,4},{6,7},{7,6},{8,9},{9,8},{10,11... | collective-permute-start | bytes 3145736 | tf_op jit(solution)/shard_map/ppermute | solution.py:12
  83.9 1.2 copy-start.2
  85.1 1.2 copy-start.3
  86.4 1.2 copy-start.5
  94.4 5.2 %copy-start.11 = (f32[128,1024]{1,0:T(8,128)S(1)}, f32[128,1024]{1,0:T(8,128)}, u32[]{:S(2)}) copy-start(f32[128,1024]{1,0:T(8,128)} %copy-done.10) | copy-start | bytes 1572868
  94.4 5.2 %copy-start.16 = (bf16[1,1024,8]{1,2,0:T(8,128)(2,1)S(1)}, bf16[1,1024,8]{1,2,0:T(8,128)(2,1)}, u32[]{:S(2)}) copy-start(bf16[1,1024,8]{1,2,0:T(8,128)(2,1)} %param.16) | copy-start | bytes 49156
  94.4 29.9 %all-to-all-start.2 = ((bf16[16,32,1024]{2,1,0:T(8,128)(2,1)}), bf16[16,32,1024]{2,1,0:T(8,128)(2,1)S(1)}, u32[]{:S(2)}, u32[]{:S(2)}) async-start(bf16[16,32,1024]{2,1,0:T(8,128)(2,1)} %bitcast.17), calls=%async_computation.2 | async-start | bytes 2097152 | tf_op jit(solution)/shard_map/all_to_all | solution.py:206
  125.1 8.2 %collective-permute-start.8 = (bf16[1,128,1024]{2,1,0:T(8,128)(2,1)S(1)}, bf16[1,128,1024]{2,1,0:T(8,128)(2,1)S(1)}, u32[]{:S(2)}, u32[]{:S(2)}) collective-permute-start(bf16[1,128,1024]{2,1,0:T(8,128)(2,1)S(1)} %fusion.12), channel_id=1, source_target_pairs={{16,0},{0,16},{17,1},{1,17},{18,2},{2,18},{19,3},{3,19},{20,4},{4,... | collective-permute-start | bytes 786440 | tf_op jit(solution)/shard_map/ppermute | solution.py:18
  (8 other events, 8.0 us)

commit v3 on v2

--- a/solution.py
+++ b/solution.py
@@ -83,10 +83,20 @@
     return jnp.broadcast_to(pages[:, None], (pages.shape[0], page_rows)).reshape(-1)
 
 
-def expert_kernel(rows_ref, gate0, up0, down0, gate1, up1, down1, out_ref, hidden_ref):
-    units = gate0.shape[1]
+def expert_kernel(rows_ref, *refs):
+    stored, (out_ref, hidden_ref), held, arrival = refs[:6], refs[6:8], refs[8:14], refs[14]
+    loads = [
+        pltpu.make_async_copy(there, here, arrival.at[i])
+        for i, (there, here) in enumerate(zip(stored, held))
+    ]
+    for load in loads:
+        load.start()
+    units = stored[0].shape[1]
     tile = 256 if units % 256 == 0 else units
-    for half, (gate_ref, up_ref, down_ref) in enumerate(((gate0, up0, down0), (gate1, up1, down1))):
+    for half in range(2):
+        gate_ref, up_ref, down_ref = held[3 * half : 3 * half + 3]
+        loads[3 * half].wait()
+        loads[3 * half + 1].wait()
         for first in range(0, units, tile):
             span = slice(first, first + tile)
             gate_act = jnp.dot(
@@ -94,6 +104,7 @@
             )
             up_act = jnp.dot(rows_ref[...], up_ref[:, span], preferred_element_type=jnp.float32)
             hidden_ref[:, span] = (jax.nn.silu(gate_act) * up_act).astype(jnp.bfloat16)
+        loads[3 * half + 2].wait()
         for first in range(0, out_ref.shape[1], tile):
             span = slice(first, first + tile)
             part = jnp.dot(
@@ -112,10 +123,13 @@
     return pl.pallas_call(
         expert_kernel,
         out_shape=jax.ShapeDtypeStruct((count, width), jnp.bfloat16),
-        in_specs=[pl.BlockSpec(memory_space=pltpu.VMEM)] * 7,
+        in_specs=[pl.BlockSpec(memory_space=pltpu.VMEM)]
+        + [pl.BlockSpec(memory_space=pl.ANY)] * 6,
         out_specs=pl.BlockSpec(memory_space=pltpu.VMEM),
-        scratch_shapes=[pltpu.VMEM((count, units), jnp.bfloat16)],
-        compiler_params=pltpu.CompilerParams(vmem_limit_bytes=32 * 1024 * 1024),
+        scratch_shapes=[pltpu.VMEM((count, units), jnp.bfloat16)]
+        + [pltpu.VMEM(weight.shape, weight.dtype) for weight in weights]
+        + [pltpu.SemaphoreType.DMA((len(weights),))],
+        compiler_params=pltpu.CompilerParams(vmem_limit_bytes=54 * 1024 * 1024),
         cost_estimate=pl.CostEstimate(
             flops=12 * count * width * units,
             bytes_accessed=12 * width * units + 4 * count * width,

time: 135 us -> 132 us (0.978)
  local copies, waits for them, and re-layouts: 18.8 us -> 9.37 us
  waiting for transfers between devices: 73.8 us -> 77.3 us
  Pallas kernels: 4.41 us -> 7.75 us
    unnamed x47 -> x29, local copies, waits for them, and re-layouts: 16 us -> 6.59 us
    ppermute x5, waiting for transfers between devices: 21.7 us -> 25.2 us  [swapped(): lax.ppermute(shard, axis, [(i, i ^ 1 << apart) for i in range(lax.axis_si...]
    pallas_call x1, Pallas kernels: 4.41 us -> 7.75 us  [whole_expert(): pl.pallas_call(expert_kernel, out_shape=jax.ShapeDtypeStruct((count, widt...]
  transfers between devices with their start and end apart: 12 -> 12, of which waited for: 8 -> 7; matrix products, arithmetic and copies ran while one was open for 10% -> 9% of each run, Pallas kernels for 0% -> 0%
where the time goes in v3:
time: 132 us; the launch traced here: 131 us
  waiting for transfers between devices  77.3 us (59%)
  starting transfers between devices  24.4 us (18%)
  matrix products  10.1 us (8%)
  local copies, waits for them, and re-layouts  9.37 us (7%)
  Pallas kernels  7.75 us (6%)
  other arithmetic  1.88 us (1%)
    ppermute x5, waiting for transfers between devices, swapped(): lax.ppermute(shard, axis, [(i, i ^ 1 << apart) for i in range(lax.axis_si...  25.2 us
    all_to_all x1, waiting for transfers between devices, shards(): lax.all_to_all(served, 'expert', split_axis=0, concat_axis=0, tiled=True)  24.5 us
    all_to_all x1, waiting for transfers between devices, shards(): lax.all_to_all(packed, 'expert', split_axis=0, concat_axis=0, tiled=True)  17.9 us
    pallas_call x1, Pallas kernels, whole_expert(): pl.pallas_call(expert_kernel, out_shape=jax.ShapeDtypeStruct((count, widt...  7.75 us
    ppermute x4, waiting for transfers between devices, from_behind(): return lax.ppermute(block, axis, route)  6.92 us
    unnamed x29, local copies, waits for them, and re-layouts  6.59 us
    all_to_all x1, starting transfers between devices, shards(): lax.all_to_all(outgoing, 'expert', split_axis=0, concat_axis=0, tiled=True)  6.16 us
    all_to_all x1, starting transfers between devices, shards(): lax.all_to_all(packed, 'expert', split_axis=0, concat_axis=0, tiled=True)  5.25 us
  transfers between devices with their start and end apart: 12, of which 7 were waited for; matrix products, arithmetic and copies ran while one was open for 9% of the time, Pallas kernels for 0%

profile of v3, /device:TPU:9, one launch (start us, length us, event | category | flops | bytes accessed | tf_op | source)
XLA Modules:
  0.0 131.2 jit_solution(13842710728444999880)
XLA Ops:
  0.0 1.3 collective-permute-start
  1.3 1.1 collective-permute-start.1
  2.4 1.4 %collective-permute-start.2 = (bf16[64,1024]{1,0:T(8,128)(2,1)}, bf16[64,1024]{1,0:T(8,128)(2,1)S(1)}, u32[]{:S(2)}, u32[]{:S(2)}) collective-permute-start(bf16[64,1024]{1,0:T(8,128)(2,1)} %bitcast.81), channel_id=1, source_target_pairs={{4,0},{5,1},{6,2},{7,3},{8,4},{9,5},{10,6},{11,7},{12,8},{13,9},{1... | collective-permute-start | bytes 393224 | tf_op jit(solution)/shard_map/ppermute | solution.py:18
  5.6 1.6 %fusion.4 = bf16[16,8,5120]{2,1,0:T(8,128)(2,1)} fusion(bf16[1,128,5120]{2,1,0:T(8,128)(2,1)S(1)} %copy-done, s32[128]{0:T(128)S(1)} %fusion.78, s32[16,8]{1,0:T(8,128)S(1)} %multiply_add_fusion.1), kind=kOutput, calls=%fused_computation.5 | convolution fusion | flops 167788544 | bytes 2622464 | tf_op jit(solution)/shard_map/dot_general | solution.py:182
  7.3 6.2 %all-to-all-start = ((bf16[16,8,5120]{2,1,0:T(8,128)(2,1)}), bf16[16,8,5120]{2,1,0:T(8,128)(2,1)S(1)}, u32[]{:S(2)}, u32[]{:S(2)}) async-start(bf16[16,8,5120]{2,1,0:T(8,128)(2,1)} %fusion.4), calls=%async_computation | async-start | bytes 2621440 | tf_op jit(solution)/shard_map/all_to_all | solution.py:183
  15.7 1.3 collective-permute-start.3
  18.9 20.2 %collective-permute-done.3 = bf16[256,1024]{1,0:T(8,128)(2,1)S(1)} collective-permute-done((bf16[256,1024]{1,0:T(8,128)(2,1)S(1)}, bf16[256,1024]{1,0:T(8,128)(2,1)S(1)}, u32[]{:S(2)}, u32[]{:S(2)}) %collective-permute-start.3) | collective-permute-done | bytes 524320 | tf_op jit(solution)/shard_map/ppermute | solution.py:12
  40.8 2.8 %all-to-all-done = bf16[16,8,5120]{2,1,0:T(8,128)(2,1)S(1)} async-done(((bf16[16,8,5120]{2,1,0:T(8,128)(2,1)}), bf16[16,8,5120]{2,1,0:T(8,128)(2,1)S(1)}, u32[]{:S(2)}, u32[]{:S(2)}) %all-to-all-start) | async-done | bytes 1310752 | tf_op jit(solution)/shard_map/all_to_all | solution.py:183
  44.2 1.1 copy-done.1
  46.4 1.9 %fusion = bf16[128,1024]{1,0:T(8,128)(2,1)S(1)} fusion(s32[1024]{0:T(1024)S(1)} %fusion.65, f32[128,1024]{1,0:T(8,128)S(1)} %copy.39, bf16[128,5120]{1,0:T(8,128)(2,1)} %copy-done.1, f32[128]{0:T(128)S(1)} %add_rsqrt_fusion.1, f32[128]{0:T(128)S(1)} %broadcast_multiply_fusion), kind=kOutput, calls=%fused_computation.1 | convolution fusion | flops 270139392 | bytes 1053696 | tf_op jit(solution)/shard_map/dot_general | solution.py:195
  48.4 1.6 %fusion.39 = f32[128,1024]{1,0:T(8,128)S(1)} fusion(bf16[512,1024]{1,0:T(8,128)(2,1)} %collective-permute-done.4, bf16[128,1024]{1,0:T(8,128)(2,1)S(1)} %fusion), kind=kOutput, calls=%fused_computation.54 | convolution fusion | flops 134217728 | bytes 1703936 | tf_op jit(solution)/shard_map/dot_general | solution.py:199
  50.1 1.4 %multiply_reduce_fusion = (f32[128]{0:T(128)S(1)}, f32[128,1024]{1,0:T(8,128)S(1)}) fusion(f32[128,1024]{1,0:T(8,128)S(1)} %fusion.39, bf16[512,1024]{1,0:T(8,128)(2,1)S(1)} %copy-done.2, bf16[128,1024]{1,0:T(8,128)(2,1)S(1)} %fusion, bf16[128,5120]{1,0:T(8,128)(2,1)} %copy-done.1), kind=kOutput, calls=%fused_computation.27 | convolution fusion | flops 135135104 | bytes 2490880 | tf_op jit(solution)/shard_map/dot_general | solution.py:197
  51.4 1.5 %fusion.36 = bf16[512,1024]{1,0:T(8,128)(2,1)} fusion(s32[128]{0:T(128)S(1)} %get-tuple-element.6, s32[128]{0:T(128)S(1)} %get-tuple-element.5, f32[128,1024]{1,0:T(8,128)S(1)} %get-tuple-element.21, f32[128]{0:T(128)S(1)} %add_rsqrt_fusion), kind=kOutput, calls=%fused_computation.52 | convolution fusion | flops 134676480 | bytes 1574400 | tf_op jit(solution)/shard_map/dot_general | solution.py:215
  52.9 5.3 %all-to-all-start.1 = ((bf16[16,32,1024]{2,1,0:T(8,128)(2,1)}), bf16[16,32,1024]{2,1,0:T(8,128)(2,1)S(1)}, u32[]{:S(2)}, u32[]{:S(2)}) async-start(bf16[16,32,1024]{2,1,0:T(8,128)(2,1)} %bitcast.12), calls=%async_computation.1 | async-start | bytes 2097152 | tf_op jit(solution)/shard_map/all_to_all | solution.py:216
  59.1 2.0 %collective-permute-done.5.refs_3_ = bf16[1024,512]{1,0:T(8,128)(2,1)S(1)} collective-permute-done((bf16[1024,512]{1,0:T(8,128)(2,1)}, bf16[1024,512]{1,0:T(8,128)(2,1)S(1)}, u32[]{:S(2)}, u32[]{:S(2)}) %collective-permute-start.5) | collective-permute-done | bytes 1048608 | tf_op jit(solution)/shard_map/ppermute | solution.py:12
  61.1 3.0 %collective-permute-done.6.refs_4_ = bf16[1024,512]{1,0:T(8,128)(2,1)S(1)} collective-permute-done((bf16[1024,512]{1,0:T(8,128)(2,1)}, bf16[1024,512]{1,0:T(8,128)(2,1)S(1)}, u32[]{:S(2)}, u32[]{:S(2)}) %collective-permute-start.6) | collective-permute-done | bytes 1048608 | tf_op jit(solution)/shard_map/ppermute | solution.py:12
  64.1 1.0 copy-done.10
  65.1 17.9 %all-to-all-done.1 = bf16[16,32,1024]{2,1,0:T(8,128)(2,1)S(1)} async-done(((bf16[16,32,1024]{2,1,0:T(8,128)(2,1)}), bf16[16,32,1024]{2,1,0:T(8,128)(2,1)S(1)}, u32[]{:S(2)}, u32[]{:S(2)}) %all-to-all-start.1) | async-done | bytes 1048608 | tf_op jit(solution)/shard_map/all_to_all | solution.py:216
  83.0 1.0 copy-done.3
  84.0 7.8 %expert_pair.1 = bf16[512,1024]{1,0:T(8,128)(2,1)} custom-call(bf16[512,1024]{1,0:T(8,128)(2,1)} %bitcast.77, bf16[1024,512]{1,0:T(8,128)(2,1)} %bitcast.86, bf16[1024,512]{1,0:T(8,128)(2,1)} %bitcast.88, bf16[512,1024]{1,0:T(8,128)(2,1)} %bitcast.90, bf16[1024,512]{1,0:T(8,128)(2,1)} %copy-done.9, bf16[1024,512]{1,0:T(8,128)(2,1)} %copy-done.10, ...), custom_call_target="tpu_custom_call" | custom-call | flops 3221225472 | bytes 8388608 | tf_op jit(solution)/shard_map/expert_pair/pallas_call | solution.py:123
  91.8 5.0 %all-to-all-start.2 = ((bf16[16,32,1024]{2,1,0:T(8,128)(2,1)}), bf16[16,32,1024]{2,1,0:T(8,128)(2,1)S(1)}, u32[]{:S(2)}, u32[]{:S(2)}) async-start(bf16[16,32,1024]{2,1,0:T(8,128)(2,1)} %bitcast.78), calls=%async_computation.2 | async-start | bytes 2097152 | tf_op jit(solution)/shard_map/all_to_all | solution.py:220
  97.2 24.5 %all-to-all-done.2 = bf16[16,32,1024]{2,1,0:T(8,128)(2,1)S(1)} async-done(((bf16[16,32,1024]{2,1,0:T(8,128)(2,1)}), bf16[16,32,1024]{2,1,0:T(8,128)(2,1)S(1)}, u32[]{:S(2)}, u32[]{:S(2)}) %all-to-all-start.2) | async-done | bytes 1048608 | tf_op jit(solution)/shard_map/all_to_all | solution.py:220
  122.3 1.3 collective-permute-start.8
  123.6 6.9 %collective-permute-done.8 = bf16[1,128,1024]{2,1,0:T(8,128)(2,1)S(1)} collective-permute-done((bf16[1,128,1024]{2,1,0:T(8,128)(2,1)S(1)}, bf16[1,128,1024]{2,1,0:T(8,128)(2,1)S(1)}, u32[]{:S(2)}, u32[]{:S(2)}) %collective-permute-start.8) | collective-permute-done | bytes 262176 | tf_op jit(solution)/shard_map/ppermute | solution.py:18
  (80 shorter events, 12.0 us)
Async XLA Ops:
  0.0 5.6 %copy-start = (bf16[1,128,5120]{2,1,0:T(8,128)(2,1)S(1)}, bf16[1,128,5120]{2,1,0:T(8,128)(2,1)}, u32[]{:S(2)}) copy-start(bf16[1,128,5120]{2,1,0:T(8,128)(2,1)} %param.10) | copy-start | bytes 3932164
  0.0 15.6 %collective-permute-start = (bf16[64,1024]{1,0:T(8,128)(2,1)}, bf16[64,1024]{1,0:T(8,128)(2,1)S(1)}, u32[]{:S(2)}, u32[]{:S(2)}) collective-permute-start(bf16[64,1024]{1,0:T(8,128)(2,1)} %bitcast.79), channel_id=1, source_target_pairs={{12,0},{13,1},{14,2},{15,3},{0,4},{1,5},{2,6},{3,7},{4,8},{5,9},{6... | collective-permute-start | bytes 393224 | tf_op jit(solution)/shard_map/ppermute | solution.py:18
  1.3 14.3 %collective-permute-start.1 = (bf16[64,1024]{1,0:T(8,128)(2,1)}, bf16[64,1024]{1,0:T(8,128)(2,1)S(1)}, u32[]{:S(2)}, u32[]{:S(2)}) collective-permute-start(bf16[64,1024]{1,0:T(8,128)(2,1)} %bitcast.80), channel_id=1, source_target_pairs={{8,0},{9,1},{10,2},{11,3},{12,4},{13,5},{14,6},{15,7},{0,8},{1,9},... | collective-permute-start | bytes 393224 | tf_op jit(solution)/shard_map/ppermute | solution.py:18
  2.4 13.2 %collective-permute-start.2 = (bf16[64,1024]{1,0:T(8,128)(2,1)}, bf16[64,1024]{1,0:T(8,128)(2,1)S(1)}, u32[]{:S(2)}, u32[]{:S(2)}) collective-permute-start(bf16[64,1024]{1,0:T(8,128)(2,1)} %bitcast.81), channel_id=1, source_target_pairs={{4,0},{5,1},{6,2},{7,3},{8,4},{9,5},{10,6},{11,7},{12,8},{13,9},{1... | collective-permute-start | bytes 393224 | tf_op jit(solution)/shard_map/ppermute | solution.py:18
  7.2 6.2 %copy-start.8 = (s32[1,1,4]{2,1,0:T(1,128)S(1)}, s32[1,1,4]{2,1,0:T(1,128)}, u32[]{:S(2)}) copy-start(s32[1,1,4]{2,1,0:T(1,128)} %param.12) | copy-start | bytes 52
  7.3 6.4 %copy-start.7 = (s32[1,1,4]{2,1,0:T(1,128)S(1)}, s32[1,1,4]{2,1,0:T(1,128)}, u32[]{:S(2)}) copy-start(s32[1,1,4]{2,1,0:T(1,128)} %param.13) | copy-start | bytes 52
  7.3 6.4 %copy-start.6 = (s32[1,128,2]{1,2,0:T(2,128)S(1)}, s32[1,128,2]{1,2,0:T(2,128)}, u32[]{:S(2)}) copy-start(s32[1,128,2]{1,2,0:T(2,128)} %param.14) | copy-start | bytes 3076
  7.3 7.3 %copy-start.4 = (bf16[1,64,1024]{2,1,0:T(8,128)(2,1)S(1)}, bf16[1,64,1024]{2,1,0:T(8,128)(2,1)}, u32[]{:S(2)}) copy-start(bf16[1,64,1024]{2,1,0:T(8,128)(2,1)} %param.15) | copy-start | bytes 393220
  7.3 36.4 %all-to-all-start = ((bf16[16,8,5120]{2,1,0:T(8,128)(2,1)}), bf16[16,8,5120]{2,1,0:T(8,128)(2,1)S(1)}, u32[]{:S(2)}, u32[]{:S(2)}) async-start(bf16[16,8,5120]{2,1,0:T(8,128)(2,1)} %fusion.4), calls=%async_computation | async-start | bytes 2621440 | tf_op jit(solution)/shard_map/all_to_all | solution.py:183
  15.7 23.4 %collective-permute-start.3 = (bf16[256,1024]{1,0:T(8,128)(2,1)S(1)}, bf16[256,1024]{1,0:T(8,128)(2,1)S(1)}, u32[]{:S(2)}, u32[]{:S(2)}) collective-permute-start(bf16[256,1024]{1,0:T(8,128)(2,1)S(1)} %pad_maximum_fusion), channel_id=1, source_target_pairs={{0,2},{1,3},{2,0},{3,1},{4,6},{5,7},{6,4},{7,5},{8,10},{9,11},{10,... | collective-permute-start | bytes 1572872 | tf_op jit(solution)/shard_map/ppermute | solution.py:12
  40.0 8.5 %collective-permute-start.4 = (bf16[512,1024]{1,0:T(8,128)(2,1)}, bf16[512,1024]{1,0:T(8,128)(2,1)}, u32[]{:S(2)}, u32[]{:S(2)}) collective-permute-start(bf16[512,1024]{1,0:T(8,128)(2,1)} %constant_dynamic-update-slice_fusion), channel_id=1, source_target_pairs={{0,1},{1,0},{2,3},{3,2},{4,5},{5,4},{6,7},{7,6},{8,9},{9,8},{10,11... | collective-permute-start | bytes 3145736 | tf_op jit(solution)/shard_map/ppermute | solution.py:12
  44.2 1.1 copy-start.1
  48.4 1.7 %copy-start.2 = (bf16[512,1024]{1,0:T(8,128)(2,1)S(1)}, bf16[512,1024]{1,0:T(8,128)(2,1)}, u32[]{:S(2)}) copy-start(bf16[512,1024]{1,0:T(8,128)(2,1)} %constant_dynamic-update-slice_fusion) | copy-start | bytes 3145732
  52.9 30.1 %all-to-all-start.1 = ((bf16[16,32,1024]{2,1,0:T(8,128)(2,1)}), bf16[16,32,1024]{2,1,0:T(8,128)(2,1)S(1)}, u32[]{:S(2)}, u32[]{:S(2)}) async-start(bf16[16,32,1024]{2,1,0:T(8,128)(2,1)} %bitcast.12), calls=%async_computation.1 | async-start | bytes 2097152 | tf_op jit(solution)/shard_map/all_to_all | solution.py:216
  58.2 2.9 %collective-permute-start.5 = (bf16[1024,512]{1,0:T(8,128)(2,1)}, bf16[1024,512]{1,0:T(8,128)(2,1)S(1)}, u32[]{:S(2)}, u32[]{:S(2)}) collective-permute-start(bf16[1024,512]{1,0:T(8,128)(2,1)} %bitcast.85), channel_id=1, source_target_pairs={{0,1},{1,0},{2,3},{3,2},{4,5},{5,4},{6,7},{7,6},{8,9},{9,8},{10,11... | collective-permute-start | bytes 3145736 | tf_op jit(solution)/shard_map/ppermute | solution.py:12
  58.5 5.5 %collective-permute-start.6 = (bf16[1024,512]{1,0:T(8,128)(2,1)}, bf16[1024,512]{1,0:T(8,128)(2,1)S(1)}, u32[]{:S(2)}, u32[]{:S(2)}) collective-permute-start(bf16[1024,512]{1,0:T(8,128)(2,1)} %bitcast.87), channel_id=1, source_target_pairs={{0,1},{1,0},{2,3},{3,2},{4,5},{5,4},{6,7},{7,6},{8,9},{9,8},{10,11... | collective-permute-start | bytes 3145736 | tf_op jit(solution)/shard_map/ppermute | solution.py:12
  58.7 6.4 %collective-permute-start.7 = (bf16[512,1024]{1,0:T(8,128)(2,1)}, bf16[512,1024]{1,0:T(8,128)(2,1)}, u32[]{:S(2)}, u32[]{:S(2)}) collective-permute-start(bf16[512,1024]{1,0:T(8,128)(2,1)} %bitcast.89), channel_id=1, source_target_pairs={{0,1},{1,0},{2,3},{3,2},{4,5},{5,4},{6,7},{7,6},{8,9},{9,8},{10,11... | collective-permute-start | bytes 3145736 | tf_op jit(solution)/shard_map/ppermute | solution.py:12
  61.1 3.0 %copy-start.9 = (bf16[1024,512]{1,0:T(8,128)(2,1)}, bf16[1024,512]{1,0:T(8,128)(2,1)S(1)}, u32[]{:S(2)}) copy-start(bf16[1024,512]{1,0:T(8,128)(2,1)S(1)} %collective-permute-done.5.refs_3_) | copy-start | bytes 3145732
  64.1 1.0 copy-start.10
  83.0 1.0 copy-start.3
  91.8 5.1 %copy-start.5 = (bf16[1,1024,8]{1,2,0:T(8,128)(2,1)S(1)}, bf16[1,1024,8]{1,2,0:T(8,128)(2,1)}, u32[]{:S(2)}) copy-start(bf16[1,1024,8]{1,2,0:T(8,128)(2,1)} %param.16) | copy-start | bytes 49156
  91.8 29.8 %all-to-all-start.2 = ((bf16[16,32,1024]{2,1,0:T(8,128)(2,1)}), bf16[16,32,1024]{2,1,0:T(8,128)(2,1)S(1)}, u32[]{:S(2)}, u32[]{:S(2)}) async-start(bf16[16,32,1024]{2,1,0:T(8,128)(2,1)} %bitcast.78), calls=%async_computation.2 | async-start | bytes 2097152 | tf_op jit(solution)/shard_map/all_to_all | solution.py:220
  122.3 8.2 %collective-permute-start.8 = (bf16[1,128,1024]{2,1,0:T(8,128)(2,1)S(1)}, bf16[1,128,1024]{2,1,0:T(8,128)(2,1)S(1)}, u32[]{:S(2)}, u32[]{:S(2)}) collective-permute-start(bf16[1,128,1024]{2,1,0:T(8,128)(2,1)S(1)} %fusion.12), channel_id=1, source_target_pairs={{16,0},{0,16},{17,1},{1,17},{18,2},{2,18},{19,3},{3,19},{20,4},{4,... | collective-permute-start | bytes 786440 | tf_op jit(solution)/shard_map/ppermute | solution.py:18

commit v4 on v3

--- a/solution.py
+++ b/solution.py
@@ -1,3 +1,5 @@
+import functools
+
 import jax
 import jax.numpy as jnp
 from jax import lax
@@ -83,60 +85,141 @@
     return jnp.broadcast_to(pages[:, None], (pages.shape[0], page_rows)).reshape(-1)
 
 
-def expert_kernel(rows_ref, *refs):
-    stored, (out_ref, hidden_ref), held, arrival = refs[:6], refs[6:8], refs[8:14], refs[14]
+def expert_kernel(devices, packed_ref, *refs):
+    stored, (back_ref, rows_ref, served_ref, hidden_ref), held = refs[:6], refs[6:10], refs[10:16]
+    arrival, own_sem, send_sem, recv_sem = refs[16:]
+    me = lax.axis_index("expert")
     loads = [
         pltpu.make_async_copy(there, here, arrival.at[i])
         for i, (there, here) in enumerate(zip(stored, held))
     ]
     for load in loads:
         load.start()
+
+    def each_peer(first, last, action):
+        def step(peer, carry):
+            @pl.when(peer != me)
+            def _():
+                action(peer)
+
+            return carry
+
+        lax.fori_loop(first, last, step, 0)
+
+    def transfer(source, target, hop, peer, sender):
+        return pltpu.make_async_remote_copy(
+            src_ref=source,
+            dst_ref=target,
+            send_sem=send_sem.at[hop, peer],
+            recv_sem=recv_sem.at[hop, sender],
+            device_id={"expert": peer},
+            device_id_type=pl.DeviceIdType.MESH,
+        )
+
+    def out_to(peer):
+        return transfer(packed_ref.at[peer], rows_ref.at[me], 0, peer, me)
+
+    def back_to(peer):
+        return transfer(served_ref.at[peer], back_ref.at[me], 1, peer, me)
+
+    barrier = pltpu.get_barrier_semaphore()
+    each_peer(
+        0,
+        devices,
+        lambda peer: pl.semaphore_signal(
+            barrier, inc=1, device_id={"expert": peer}, device_id_type=pl.DeviceIdType.MESH
+        ),
+    )
+    pl.semaphore_wait(barrier, devices - 1)
+    each_peer(0, devices, lambda peer: out_to(peer).start())
+    kept = pltpu.make_async_copy(packed_ref.at[me], rows_ref.at[me], own_sem.at[0])
+    kept.start()
+    kept.wait()
     units = stored[0].shape[1]
+    width = packed_ref.shape[2]
     tile = 256 if units % 256 == 0 else units
-    for half in range(2):
-        gate_ref, up_ref, down_ref = held[3 * half : 3 * half + 3]
-        loads[3 * half].wait()
-        loads[3 * half + 1].wait()
-        for first in range(0, units, tile):
-            span = slice(first, first + tile)
-            gate_act = jnp.dot(
-                rows_ref[...], gate_ref[:, span], preferred_element_type=jnp.float32
-            )
-            up_act = jnp.dot(rows_ref[...], up_ref[:, span], preferred_element_type=jnp.float32)
-            hidden_ref[:, span] = (jax.nn.silu(gate_act) * up_act).astype(jnp.bfloat16)
-        loads[3 * half + 2].wait()
-        for first in range(0, out_ref.shape[1], tile):
-            span = slice(first, first + tile)
-            part = jnp.dot(
-                hidden_ref[...], down_ref[:, span], preferred_element_type=jnp.float32
-            ).astype(jnp.bfloat16)
-            if half == 0:
-                out_ref[:, span] = part
-            else:
-                earlier = out_ref[:, span].astype(jnp.float32)
-                out_ref[:, span] = (earlier + part.astype(jnp.float32)).astype(jnp.bfloat16)
-
-
-def whole_expert(rows, *weights):
-    count, width = rows.shape
+    group = devices // 2
+    for turn in range(2):
+        begin = turn * group
+        each_peer(
+            begin,
+            begin + group,
+            lambda peer: transfer(packed_ref.at[peer], rows_ref.at[peer], 0, peer, peer).wait_recv(),
+        )
+        rows = rows_ref[begin : begin + group].reshape(-1, width)
+        for half in range(2):
+            gate_ref, up_ref, down_ref = held[3 * half : 3 * half + 3]
+            if turn == 0:
+                loads[3 * half].wait()
+                loads[3 * half + 1].wait()
+            for first in range(0, units, tile):
+                span = slice(first, first + tile)
+                gate_act = jnp.dot(rows, gate_ref[:, span], preferred_element_type=jnp.float32)
+                up_act = jnp.dot(rows, up_ref[:, span], preferred_element_type=jnp.float32)
+                hidden_ref[:, span] = (jax.nn.silu(gate_act) * up_act).astype(jnp.bfloat16)
+            if turn == 0:
+                loads[3 * half + 2].wait()
+            for first in range(0, width, tile):
+                span = slice(first, first + tile)
+                part = jnp.dot(
+                    hidden_ref[...], down_ref[:, span], preferred_element_type=jnp.float32
+                ).astype(jnp.bfloat16)
+                part = part.reshape(group, -1, tile)
+                if half == 0:
+                    served_ref[begin : begin + group, :, span] = part
+                else:
+                    earlier = served_ref[begin : begin + group, :, span].astype(jnp.float32)
+                    served_ref[begin : begin + group, :, span] = (
+                        earlier + part.astype(jnp.float32)
+                    ).astype(jnp.bfloat16)
+        each_peer(begin, begin + group, lambda peer: back_to(peer).start())
+    kept = pltpu.make_async_copy(served_ref.at[me], back_ref.at[me], own_sem.at[1])
+    kept.start()
+    kept.wait()
+    each_peer(0, devices, lambda peer: out_to(peer).wait_send())
+    each_peer(0, devices, lambda peer: back_to(peer).wait_send())
+    each_peer(
+        0,
+        devices,
+        lambda peer: transfer(served_ref.at[peer], back_ref.at[peer], 1, peer, peer).wait_recv(),
+    )
+
+
+def exchanged_experts(packed, *weights):
+    devices = lax.axis_size("expert")
+    width = packed.shape[1]
+    blocks = packed.reshape(devices, -1, width)
+    count = packed.shape[0]
     units = weights[0].shape[1]
-    return pl.pallas_call(
-        expert_kernel,
-        out_shape=jax.ShapeDtypeStruct((count, width), jnp.bfloat16),
+    came_back = pl.pallas_call(
+        functools.partial(expert_kernel, devices),
+        out_shape=jax.ShapeDtypeStruct(blocks.shape, jnp.bfloat16),
         in_specs=[pl.BlockSpec(memory_space=pltpu.VMEM)]
         + [pl.BlockSpec(memory_space=pl.ANY)] * 6,
         out_specs=pl.BlockSpec(memory_space=pltpu.VMEM),
-        scratch_shapes=[pltpu.VMEM((count, units), jnp.bfloat16)]
+        scratch_shapes=[
+            pltpu.VMEM(blocks.shape, jnp.bfloat16),
+            pltpu.VMEM(blocks.shape, jnp.bfloat16),
+            pltpu.VMEM((count // 2, units), jnp.bfloat16),
+        ]
         + [pltpu.VMEM(weight.shape, weight.dtype) for weight in weights]
-        + [pltpu.SemaphoreType.DMA((len(weights),))],
-        compiler_params=pltpu.CompilerParams(vmem_limit_bytes=54 * 1024 * 1024),
+        + [
+            pltpu.SemaphoreType.DMA((len(weights),)),
+            pltpu.SemaphoreType.DMA((2,)),
+            pltpu.SemaphoreType.DMA((2, devices)),
+            pltpu.SemaphoreType.DMA((2, devices)),
+        ],
+        compiler_params=pltpu.CompilerParams(
+            vmem_limit_bytes=54 * 1024 * 1024, collective_id=0, has_side_effects=True
+        ),
         cost_estimate=pl.CostEstimate(
             flops=12 * count * width * units,
             bytes_accessed=12 * width * units + 4 * count * width,
             transcendentals=2 * count * units,
         ),
-        name="expert_pair",
-    )(rows, *weights)
+        name="expert_exchange",
+    )(blocks, *weights)
+    return came_back.reshape(count, width)
 
 
 def gathered_projection(block):
@@ -213,11 +296,9 @@
         (slots[None, :, 0] == slot_index[:, None]) | (slots[None, :, 1] == slot_index[:, None])
     ).astype(jnp.bfloat16)
     packed = jnp.dot(packing, normed)
-    own_rows = lax.all_to_all(packed, "expert", split_axis=0, concat_axis=0, tiled=True)
-    served = whole_expert(
-        own_rows, w_gate[0], w_up[0], w_down[0], other_gate, other_up, other_down
-    )
-    came_back = lax.all_to_all(served, "expert", split_axis=0, concat_axis=0, tiled=True)
+    came_back = exchanged_experts(
+        packed, w_gate[0], w_up[0], w_down[0], other_gate, other_up, other_down
+    )
     mixture = jnp.zeros_like(resid_wide)
     for k in range(slots.shape[1]):
         picking = (slots[:, k : k + 1] == slot_index[None, :]).astype(jnp.bfloat16)

time: 132 us -> 118 us (0.89)
  waiting for transfers between devices: 77.3 us -> 29.1 us
  Pallas kernels: 7.75 us -> 53.2 us
  starting transfers between devices: 24.4 us -> 14 us
  local copies, waits for them, and re-layouts: 9.37 us -> 7.38 us
    pallas_call x1, Pallas kernels: 7.75 us -> 53.2 us  [exchanged_experts(): pl.pallas_call(functools.partial(expert_kernel, devices), out_shape=jax.S...]
    all_to_all x2 -> x0, waiting for transfers between devices: 42.4 us -> none  [the longest x1 24.5 us: shards(): lax.all_to_all(served, 'expert', split_axis=0, concat_axis=0, tiled=True)]
    all_to_all x2 -> x0, starting transfers between devices: 10.2 us -> none  [the longest x1 5.25 us: shards(): lax.all_to_all(packed, 'expert', split_axis=0, concat_axis=0, tiled=True)]
    ppermute x5, waiting for transfers between devices: 25.2 us -> 19.5 us  [swapped(): lax.ppermute(shard, axis, [(i, i ^ 1 << apart) for i in range(lax.axis_si...]
    unnamed x29 -> x25, local copies, waits for them, and re-layouts: 6.59 us -> 4.6 us
  transfers between devices with their start and end apart: 12 -> 10, of which waited for: 7 -> 3; matrix products, arithmetic and copies ran while one was open for 9% -> 14% of each run, Pallas kernels for 0% -> 0%
where the time goes in v4:
time: 118 us; the launch traced here: 117 us
  Pallas kernels  53.2 us (45%)
  waiting for transfers between devices  29.1 us (25%)
  starting transfers between devices  14 us (12%)
  matrix products  11.4 us (10%)
  local copies, waits for them, and re-layouts  7.38 us (6%)
  other arithmetic  1.88 us (2%)
    pallas_call x1, Pallas kernels, exchanged_experts(): pl.pallas_call(functools.partial(expert_kernel, devices), out_shape=jax.S...  53.2 us
    ppermute x5, waiting for transfers between devices, swapped(): lax.ppermute(shard, axis, [(i, i ^ 1 << apart) for i in range(lax.axis_si...  19.5 us
    ppermute x4, waiting for transfers between devices, from_behind(): return lax.ppermute(block, axis, route)  6.78 us
    all_to_all x1, starting transfers between devices, shards(): lax.all_to_all(outgoing, 'expert', split_axis=0, concat_axis=0, tiled=True)  6.16 us
    ppermute x4, starting transfers between devices, from_behind(): return lax.ppermute(block, axis, route)  5.06 us
    unnamed x25, local copies, waits for them, and re-layouts  4.6 us
    all_to_all x1, waiting for transfers between devices, shards(): lax.all_to_all(outgoing, 'expert', split_axis=0, concat_axis=0, tiled=True)  2.81 us
    ppermute x5, starting transfers between devices, swapped(): lax.ppermute(shard, axis, [(i, i ^ 1 << apart) for i in range(lax.axis_si...  2.75 us
  transfers between devices with their start and end apart: 10, of which 3 were waited for; matrix products, arithmetic and copies ran while one was open for 14% of the time, Pallas kernels for 0%

profile of v4, /device:TPU:9, one launch (start us, length us, event | category | flops | bytes accessed | tf_op | source)
XLA Modules:
  0.0 117.3 jit_solution(4026132439214822594)
XLA Ops:
  0.0 1.3 %collective-permute-start = (bf16[64,1024]{1,0:T(8,128)(2,1)}, bf16[64,1024]{1,0:T(8,128)(2,1)S(1)}, u32[]{:S(2)}, u32[]{:S(2)}) collective-permute-start(bf16[64,1024]{1,0:T(8,128)(2,1)} %bitcast.76), channel_id=1, source_target_pairs={{12,0},{13,1},{14,2},{15,3},{0,4},{1,5},{2,6},{3,7},{4,8},{5,9},{6... | collective-permute-start | bytes 393224 | tf_op jit(solution)/shard_map/ppermute | solution.py:20
  1.3 1.1 collective-permute-start.1
  2.4 1.4 %collective-permute-start.2 = (bf16[64,1024]{1,0:T(8,128)(2,1)}, bf16[64,1024]{1,0:T(8,128)(2,1)S(1)}, u32[]{:S(2)}, u32[]{:S(2)}) collective-permute-start(bf16[64,1024]{1,0:T(8,128)(2,1)} %bitcast.78), channel_id=1, source_target_pairs={{4,0},{5,1},{6,2},{7,3},{8,4},{9,5},{10,6},{11,7},{12,8},{13,9},{1... | collective-permute-start | bytes 393224 | tf_op jit(solution)/shard_map/ppermute | solution.py:20
  3.8 0.8 and_select_fusion.3
  4.5 0.7 slice_bitcast_fusion.4
  5.6 1.6 %fusion.4 = bf16[16,8,5120]{2,1,0:T(8,128)(2,1)} fusion(bf16[1,128,5120]{2,1,0:T(8,128)(2,1)S(1)} %copy-done, s32[128]{0:T(128)S(1)} %fusion.78, s32[16,8]{1,0:T(8,128)S(1)} %multiply_add_fusion.1), kind=kOutput, calls=%fused_computation.5 | convolution fusion | flops 167788544 | bytes 2622464 | tf_op jit(solution)/shard_map/dot_general | solution.py:265
  7.3 6.2 %all-to-all-start = ((bf16[16,8,5120]{2,1,0:T(8,128)(2,1)}), bf16[16,8,5120]{2,1,0:T(8,128)(2,1)S(1)}, u32[]{:S(2)}, u32[]{:S(2)}) async-start(bf16[16,8,5120]{2,1,0:T(8,128)(2,1)} %fusion.4), calls=%async_computation | async-start | bytes 2621440 | tf_op jit(solution)/shard_map/all_to_all | solution.py:266
  15.0 0.7 constant_dynamic-update-slice_fusion.4
  16.7 1.3 %collective-permute-start.3 = (bf16[256,1024]{1,0:T(8,128)(2,1)S(1)}, bf16[256,1024]{1,0:T(8,128)(2,1)S(1)}, u32[]{:S(2)}, u32[]{:S(2)}) collective-permute-start(bf16[256,1024]{1,0:T(8,128)(2,1)S(1)} %pad_maximum_fusion), channel_id=1, source_target_pairs={{0,2},{1,3},{2,0},{3,1},{4,6},{5,7},{6,4},{7,5},{8,10},{9,11},{10,... | collective-permute-start | bytes 1572872 | tf_op jit(solution)/shard_map/ppermute | solution.py:14
  17.9 0.7 constant_dynamic-update-slice_fusion.3
  18.6 0.7 constant_dynamic-update-slice_fusion.2
  19.9 19.5 %collective-permute-done.3 = bf16[256,1024]{1,0:T(8,128)(2,1)S(1)} collective-permute-done((bf16[256,1024]{1,0:T(8,128)(2,1)S(1)}, bf16[256,1024]{1,0:T(8,128)(2,1)S(1)}, u32[]{:S(2)}, u32[]{:S(2)}) %collective-permute-start.3) | collective-permute-done | bytes 524320 | tf_op jit(solution)/shard_map/ppermute | solution.py:14
  39.4 0.8 constant_dynamic-update-slice_fusion
  40.8 2.8 %all-to-all-done = bf16[16,8,5120]{2,1,0:T(8,128)(2,1)S(1)} async-done(((bf16[16,8,5120]{2,1,0:T(8,128)(2,1)}), bf16[16,8,5120]{2,1,0:T(8,128)(2,1)S(1)}, u32[]{:S(2)}, u32[]{:S(2)}) %all-to-all-start) | async-done | bytes 1310752 | tf_op jit(solution)/shard_map/all_to_all | solution.py:266
  44.2 1.1 copy-done.1
  46.4 1.9 %fusion = bf16[128,1024]{1,0:T(8,128)(2,1)S(1)} fusion(s32[1024]{0:T(1024)S(1)} %fusion.65, f32[128,1024]{1,0:T(8,128)S(1)} %copy.39, bf16[128,5120]{1,0:T(8,128)(2,1)} %copy-done.1, f32[128]{0:T(128)S(1)} %add_rsqrt_fusion.1, f32[128]{0:T(128)S(1)} %broadcast_multiply_fusion), kind=kOutput, calls=%fused_computation.1 | convolution fusion | flops 270139392 | bytes 1053696 | tf_op jit(solution)/shard_map/dot_general | solution.py:278
  48.4 1.6 %fusion.39 = f32[128,1024]{1,0:T(8,128)S(1)} fusion(bf16[512,1024]{1,0:T(8,128)(2,1)} %collective-permute-done.4, bf16[128,1024]{1,0:T(8,128)(2,1)S(1)} %fusion), kind=kOutput, calls=%fused_computation.54 | convolution fusion | flops 134217728 | bytes 1703936 | tf_op jit(solution)/shard_map/dot_general | solution.py:282
  50.1 1.4 %multiply_reduce_fusion = (f32[128]{0:T(128)S(1)}, f32[128,1024]{1,0:T(8,128)S(1)}) fusion(f32[128,1024]{1,0:T(8,128)S(1)} %fusion.39, bf16[512,1024]{1,0:T(8,128)(2,1)S(1)} %copy-done.3, bf16[128,1024]{1,0:T(8,128)(2,1)S(1)} %fusion, bf16[128,5120]{1,0:T(8,128)(2,1)} %copy-done.1), kind=kOutput, calls=%fused_computation.27 | convolution fusion | flops 135135104 | bytes 2490880 | tf_op jit(solution)/shard_map/dot_general | solution.py:280
  51.8 1.5 %fusion.36 = bf16[512,1024]{1,0:T(8,128)(2,1)} fusion(s32[128]{0:T(128)S(1)} %get-tuple-element.6, s32[128]{0:T(128)S(1)} %get-tuple-element.5, f32[128,1024]{1,0:T(8,128)S(1)} %get-tuple-element.21, f32[128]{0:T(128)S(1)} %add_rsqrt_fusion), kind=kOutput, calls=%fused_computation.52 | convolution fusion | flops 134676480 | bytes 1574400 | tf_op jit(solution)/shard_map/dot_general | solution.py:298
  53.3 53.2 %expert_exchange.1 = bf16[16,32,1024]{2,1,0:T(8,128)(2,1)} custom-call(bf16[16,32,1024]{2,1,0:T(8,128)(2,1)} %bitcast.74, bf16[1024,512]{1,0:T(8,128)(2,1)} %bitcast.83, bf16[1024,512]{1,0:T(8,128)(2,1)} %bitcast.85, bf16[512,1024]{1,0:T(8,128)(2,1)} %bitcast.87, bf16[1024,512]{1,0:T(8,128)(2,1)} %collective-permute-done.5.refs_3_, ...), custom_call_target="tpu_custom_call" | custom-call | flops 3221225472 | bytes 8388608 | tf_op jit(solution)/shard_map/expert_exchange/pallas_call | solution.py:194
  106.5 1.7 %convolution_multiply_fusion = f32[128,1024]{1,0:T(8,128)S(1)} fusion(bf16[512,1024]{1,0:T(8,128)(2,1)} %bitcast.71, f32[128]{0:T(128)S(1)} %get-tuple-element.15, s32[128]{0:T(128)S(1)} %get-tuple-element.6), kind=kOutput, calls=%fused_computation.9 | convolution fusion | flops 134414336 | bytes 1573888 | tf_op jit(solution)/shard_map/dot_general | solution.py:305
  108.5 1.3 %collective-permute-start.8 = (bf16[1,128,1024]{2,1,0:T(8,128)(2,1)S(1)}, bf16[1,128,1024]{2,1,0:T(8,128)(2,1)S(1)}, u32[]{:S(2)}, u32[]{:S(2)}) collective-permute-start(bf16[1,128,1024]{2,1,0:T(8,128)(2,1)S(1)} %fusion.12), channel_id=1, source_target_pairs={{16,0},{0,16},{17,1},{1,17},{18,2},{2,18},{19,3},{3,19},{20,4},{4,... | collective-permute-start | bytes 786440 | tf_op jit(solution)/shard_map/ppermute | solution.py:20
  109.8 6.8 %collective-permute-done.8 = bf16[1,128,1024]{2,1,0:T(8,128)(2,1)S(1)} collective-permute-done((bf16[1,128,1024]{2,1,0:T(8,128)(2,1)S(1)}, bf16[1,128,1024]{2,1,0:T(8,128)(2,1)S(1)}, u32[]{:S(2)}, u32[]{:S(2)}) %collective-permute-start.8) | collective-permute-done | bytes 262176 | tf_op jit(solution)/shard_map/ppermute | solution.py:20
  116.6 0.7 copy.61
  (72 shorter events, 6.5 us)
Async XLA Ops:
  0.0 5.6 %copy-start = (bf16[1,128,5120]{2,1,0:T(8,128)(2,1)S(1)}, bf16[1,128,5120]{2,1,0:T(8,128)(2,1)}, u32[]{:S(2)}) copy-start(bf16[1,128,5120]{2,1,0:T(8,128)(2,1)} %param.10) | copy-start | bytes 3932164
  0.0 16.2 %collective-permute-start = (bf16[64,1024]{1,0:T(8,128)(2,1)}, bf16[64,1024]{1,0:T(8,128)(2,1)S(1)}, u32[]{:S(2)}, u32[]{:S(2)}) collective-permute-start(bf16[64,1024]{1,0:T(8,128)(2,1)} %bitcast.76), channel_id=1, source_target_pairs={{12,0},{13,1},{14,2},{15,3},{0,4},{1,5},{2,6},{3,7},{4,8},{5,9},{6... | collective-permute-start | bytes 393224 | tf_op jit(solution)/shard_map/ppermute | solution.py:20
  1.3 15.3 %collective-permute-start.1 = (bf16[64,1024]{1,0:T(8,128)(2,1)}, bf16[64,1024]{1,0:T(8,128)(2,1)S(1)}, u32[]{:S(2)}, u32[]{:S(2)}) collective-permute-start(bf16[64,1024]{1,0:T(8,128)(2,1)} %bitcast.77), channel_id=1, source_target_pairs={{8,0},{9,1},{10,2},{11,3},{12,4},{13,5},{14,6},{15,7},{0,8},{1,9},... | collective-permute-start | bytes 393224 | tf_op jit(solution)/shard_map/ppermute | solution.py:20
  2.4 14.2 %collective-permute-start.2 = (bf16[64,1024]{1,0:T(8,128)(2,1)}, bf16[64,1024]{1,0:T(8,128)(2,1)S(1)}, u32[]{:S(2)}, u32[]{:S(2)}) collective-permute-start(bf16[64,1024]{1,0:T(8,128)(2,1)} %bitcast.78), channel_id=1, source_target_pairs={{4,0},{5,1},{6,2},{7,3},{8,4},{9,5},{10,6},{11,7},{12,8},{13,9},{1... | collective-permute-start | bytes 393224 | tf_op jit(solution)/shard_map/ppermute | solution.py:20
  7.2 6.7 %copy-start.8 = (s32[1,1,4]{2,1,0:T(1,128)S(1)}, s32[1,1,4]{2,1,0:T(1,128)}, u32[]{:S(2)}) copy-start(s32[1,1,4]{2,1,0:T(1,128)} %param.12) | copy-start | bytes 52
  7.3 6.9 %copy-start.7 = (s32[1,1,4]{2,1,0:T(1,128)S(1)}, s32[1,1,4]{2,1,0:T(1,128)}, u32[]{:S(2)}) copy-start(s32[1,1,4]{2,1,0:T(1,128)} %param.13) | copy-start | bytes 52
  7.3 6.9 %copy-start.6 = (s32[1,128,2]{1,2,0:T(2,128)S(1)}, s32[1,128,2]{1,2,0:T(2,128)}, u32[]{:S(2)}) copy-start(s32[1,128,2]{1,2,0:T(2,128)} %param.14) | copy-start | bytes 3076
  7.3 7.8 %copy-start.4 = (bf16[1,64,1024]{2,1,0:T(8,128)(2,1)S(1)}, bf16[1,64,1024]{2,1,0:T(8,128)(2,1)}, u32[]{:S(2)}) copy-start(bf16[1,64,1024]{2,1,0:T(8,128)(2,1)} %param.15) | copy-start | bytes 393220
  7.3 36.4 %all-to-all-start = ((bf16[16,8,5120]{2,1,0:T(8,128)(2,1)}), bf16[16,8,5120]{2,1,0:T(8,128)(2,1)S(1)}, u32[]{:S(2)}, u32[]{:S(2)}) async-start(bf16[16,8,5120]{2,1,0:T(8,128)(2,1)} %fusion.4), calls=%async_computation | async-start | bytes 2621440 | tf_op jit(solution)/shard_map/all_to_all | solution.py:266
  13.4 39.8 %collective-permute-start.5 = (bf16[1024,512]{1,0:T(8,128)(2,1)}, bf16[1024,512]{1,0:T(8,128)(2,1)}, u32[]{:S(2)}, u32[]{:S(2)}) collective-permute-start(bf16[1024,512]{1,0:T(8,128)(2,1)} %bitcast.82), channel_id=1, source_target_pairs={{0,1},{1,0},{2,3},{3,2},{4,5},{5,4},{6,7},{7,6},{8,9},{9,8},{10,11... | collective-permute-start | bytes 3145736 | tf_op jit(solution)/shard_map/ppermute | solution.py:14
  13.8 39.5 %collective-permute-start.6 = (bf16[1024,512]{1,0:T(8,128)(2,1)}, bf16[1024,512]{1,0:T(8,128)(2,1)}, u32[]{:S(2)}, u32[]{:S(2)}) collective-permute-start(bf16[1024,512]{1,0:T(8,128)(2,1)} %bitcast.84), channel_id=1, source_target_pairs={{0,1},{1,0},{2,3},{3,2},{4,5},{5,4},{6,7},{7,6},{8,9},{9,8},{10,11... | collective-permute-start | bytes 3145736 | tf_op jit(solution)/shard_map/ppermute | solution.py:14
  16.2 37.1 %collective-permute-start.7 = (bf16[512,1024]{1,0:T(8,128)(2,1)}, bf16[512,1024]{1,0:T(8,128)(2,1)}, u32[]{:S(2)}, u32[]{:S(2)}) collective-permute-start(bf16[512,1024]{1,0:T(8,128)(2,1)} %bitcast.86), channel_id=1, source_target_pairs={{0,1},{1,0},{2,3},{3,2},{4,5},{5,4},{6,7},{7,6},{8,9},{9,8},{10,11... | collective-permute-start | bytes 3145736 | tf_op jit(solution)/shard_map/ppermute | solution.py:14
  16.7 22.8 %collective-permute-start.3 = (bf16[256,1024]{1,0:T(8,128)(2,1)S(1)}, bf16[256,1024]{1,0:T(8,128)(2,1)S(1)}, u32[]{:S(2)}, u32[]{:S(2)}) collective-permute-start(bf16[256,1024]{1,0:T(8,128)(2,1)S(1)} %pad_maximum_fusion), channel_id=1, source_target_pairs={{0,2},{1,3},{2,0},{3,1},{4,6},{5,7},{6,4},{7,5},{8,10},{9,11},{10,... | collective-permute-start | bytes 1572872 | tf_op jit(solution)/shard_map/ppermute | solution.py:14
  40.3 8.1 %collective-permute-start.4 = (bf16[512,1024]{1,0:T(8,128)(2,1)}, bf16[512,1024]{1,0:T(8,128)(2,1)}, u32[]{:S(2)}, u32[]{:S(2)}) collective-permute-start(bf16[512,1024]{1,0:T(8,128)(2,1)} %constant_dynamic-update-slice_fusion), channel_id=1, source_target_pairs={{0,1},{1,0},{2,3},{3,2},{4,5},{5,4},{6,7},{7,6},{8,9},{9,8},{10,11... | collective-permute-start | bytes 3145736 | tf_op jit(solution)/shard_map/ppermute | solution.py:14
  44.2 1.1 copy-start.1
  48.4 1.6 %copy-start.3 = (bf16[512,1024]{1,0:T(8,128)(2,1)S(1)}, bf16[512,1024]{1,0:T(8,128)(2,1)}, u32[]{:S(2)}) copy-start(bf16[512,1024]{1,0:T(8,128)(2,1)} %constant_dynamic-update-slice_fusion) | copy-start | bytes 3145732
  50.1 1.4 %copy-start.5 = (bf16[1,1024,8]{1,2,0:T(8,128)(2,1)S(1)}, bf16[1,1024,8]{1,2,0:T(8,128)(2,1)}, u32[]{:S(2)}) copy-start(bf16[1,1024,8]{1,2,0:T(8,128)(2,1)} %param.16) | copy-start | bytes 49156
  106.5 1.7 %copy-start.2 = (bf16[16,32,1024]{2,1,0:T(8,128)(2,1)S(1)}, bf16[16,32,1024]{2,1,0:T(8,128)(2,1)}, u32[]{:S(2)}) copy-start(bf16[16,32,1024]{2,1,0:T(8,128)(2,1)} %expert_exchange.1) | copy-start | bytes 3145732
  108.5 8.1 %collective-permute-start.8 = (bf16[1,128,1024]{2,1,0:T(8,128)(2,1)S(1)}, bf16[1,128,1024]{2,1,0:T(8,128)(2,1)S(1)}, u32[]{:S(2)}, u32[]{:S(2)}) collective-permute-start(bf16[1,128,1024]{2,1,0:T(8,128)(2,1)S(1)} %fusion.12), channel_id=1, source_target_pairs={{16,0},{0,16},{17,1},{1,17},{18,2},{2,18},{19,3},{3,19},{20,4},{4,... | collective-permute-start | bytes 786440 | tf_op jit(solution)/shard_map/ppermute | solution.py:20

commit v5 on v4

--- a/solution.py
+++ b/solution.py
@@ -96,15 +96,25 @@
     for load in loads:
         load.start()
 
-    def each_peer(first, last, action):
-        def step(peer, carry):
+    group = devices // 2
+    near = (me // group) * group
+    far = group - near
+
+    def each_peer(first, action):
+        def step(k, carry):
+            peer = first + lax.rem(me + k, group)
+
             @pl.when(peer != me)
             def _():
                 action(peer)
 
             return carry
 
-        lax.fori_loop(first, last, step, 0)
+        lax.fori_loop(0, group, step, 0)
+
+    def everyone(action):
+        each_peer(far, action)
+        each_peer(near, action)
 
     def transfer(source, target, hop, peer, sender):
         return pltpu.make_async_remote_copy(
@@ -123,30 +133,26 @@
         return transfer(served_ref.at[peer], back_ref.at[me], 1, peer, me)
 
     barrier = pltpu.get_barrier_semaphore()
-    each_peer(
-        0,
-        devices,
+    everyone(
         lambda peer: pl.semaphore_signal(
             barrier, inc=1, device_id={"expert": peer}, device_id_type=pl.DeviceIdType.MESH
-        ),
+        )
     )
     pl.semaphore_wait(barrier, devices - 1)
-    each_peer(0, devices, lambda peer: out_to(peer).start())
+    everyone(lambda peer: out_to(peer).start())
     kept = pltpu.make_async_copy(packed_ref.at[me], rows_ref.at[me], own_sem.at[0])
     kept.start()
     kept.wait()
     units = stored[0].shape[1]
     width = packed_ref.shape[2]
     tile = 256 if units % 256 == 0 else units
-    group = devices // 2
     for turn in range(2):
-        begin = turn * group
+        begin = near if turn == 0 else far
         each_peer(
             begin,
-            begin + group,
             lambda peer: transfer(packed_ref.at[peer], rows_ref.at[peer], 0, peer, peer).wait_recv(),
         )
-        rows = rows_ref[begin : begin + group].reshape(-1, width)
+        rows = rows_ref[pl.ds(begin, group)].reshape(-1, width)
         for half in range(2):
             gate_ref, up_ref, down_ref = held[3 * half : 3 * half + 3]
             if turn == 0:
@@ -166,22 +172,20 @@
                 ).astype(jnp.bfloat16)
                 part = part.reshape(group, -1, tile)
                 if half == 0:
-                    served_ref[begin : begin + group, :, span] = part
+                    served_ref[pl.ds(begin, group), :, span] = part
                 else:
-                    earlier = served_ref[begin : begin + group, :, span].astype(jnp.float32)
-                    served_ref[begin : begin + group, :, span] = (
+                    earlier = served_ref[pl.ds(begin, group), :, span].astype(jnp.float32)
+                    served_ref[pl.ds(begin, group), :, span] = (
                         earlier + part.astype(jnp.float32)
                     ).astype(jnp.bfloat16)
-        each_peer(begin, begin + group, lambda peer: back_to(peer).start())
+        each_peer(begin, lambda peer: back_to(peer).start())
     kept = pltpu.make_async_copy(served_ref.at[me], back_ref.at[me], own_sem.at[1])
     kept.start()
     kept.wait()
-    each_peer(0, devices, lambda peer: out_to(peer).wait_send())
-    each_peer(0, devices, lambda peer: back_to(peer).wait_send())
-    each_peer(
-        0,
-        devices,
-        lambda peer: transfer(served_ref.at[peer], back_ref.at[peer], 1, peer, peer).wait_recv(),
+    everyone(lambda peer: out_to(peer).wait_send())
+    everyone(lambda peer: back_to(peer).wait_send())
+    everyone(
+        lambda peer: transfer(served_ref.at[peer], back_ref.at[peer], 1, peer, peer).wait_recv()
     )
 
 

time: 118 us -> 121 us (1.025)
  the two profiles are of different devices: /device:TPU:9 before, /device:TPU:0 now
where the time goes in v5:
time: 121 us; the launch traced here: 120 us
  Pallas kernels  55.4 us (46%)
  waiting for transfers between devices  28.9 us (24%)
  starting transfers between devices  15 us (12%)
  matrix products  11.4 us (9%)
  local copies, waits for them, and re-layouts  7.38 us (6%)
  other arithmetic  1.88 us (2%)
    pallas_call x1, Pallas kernels, exchanged_experts(): pl.pallas_call(functools.partial(expert_kernel, devices), out_shape=jax.S...  55.4 us
    ppermute x5, waiting for transfers between devices, swapped(): lax.ppermute(shard, axis, [(i, i ^ 1 << apart) for i in range(lax.axis_si...  21.3 us
    ppermute x4, starting transfers between devices, from_behind(): return lax.ppermute(block, axis, route)  8.51 us
    ppermute x4, waiting for transfers between devices, from_behind(): return lax.ppermute(block, axis, route)  7.53 us
    unnamed x25, local copies, waits for them, and re-layouts  4.6 us
    all_to_all x1, starting transfers between devices, shards(): lax.all_to_all(outgoing, 'expert', split_axis=0, concat_axis=0, tiled=True)  3.84 us
    ppermute x5, starting transfers between devices, swapped(): lax.ppermute(shard, axis, [(i, i ^ 1 << apart) for i in range(lax.axis_si...  2.62 us
  transfers between devices with their start and end apart: 10, of which 2 were waited for; matrix products, arithmetic and copies ran while one was open for 14% of the time, Pallas kernels for 0%

profile of v5, /device:TPU:0, one launch (start us, length us, event | category | flops | bytes accessed | tf_op | source)
XLA Modules:
  0.0 120.3 jit_solution(15863720976376526839)
XLA Ops:
  0.0 3.0 %collective-permute-start = (bf16[64,1024]{1,0:T(8,128)(2,1)}, bf16[64,1024]{1,0:T(8,128)(2,1)S(1)}, u32[]{:S(2)}, u32[]{:S(2)}) collective-permute-start(bf16[64,1024]{1,0:T(8,128)(2,1)} %bitcast.76), channel_id=1, source_target_pairs={{12,0},{13,1},{14,2},{15,3},{0,4},{1,5},{2,6},{3,7},{4,8},{5,9},{6... | collective-permute-start | bytes 393224 | tf_op jit(solution)/shard_map/ppermute | solution.py:20
  3.0 2.6 %collective-permute-start.1 = (bf16[64,1024]{1,0:T(8,128)(2,1)}, bf16[64,1024]{1,0:T(8,128)(2,1)S(1)}, u32[]{:S(2)}, u32[]{:S(2)}) collective-permute-start(bf16[64,1024]{1,0:T(8,128)(2,1)} %bitcast.77), channel_id=1, source_target_pairs={{8,0},{9,1},{10,2},{11,3},{12,4},{13,5},{14,6},{15,7},{0,8},{1,9},... | collective-permute-start | bytes 393224 | tf_op jit(solution)/shard_map/ppermute | solution.py:20
  5.6 1.3 %collective-permute-start.2 = (bf16[64,1024]{1,0:T(8,128)(2,1)}, bf16[64,1024]{1,0:T(8,128)(2,1)S(1)}, u32[]{:S(2)}, u32[]{:S(2)}) collective-permute-start(bf16[64,1024]{1,0:T(8,128)(2,1)} %bitcast.78), channel_id=1, source_target_pairs={{4,0},{5,1},{6,2},{7,3},{8,4},{9,5},{10,6},{11,7},{12,8},{13,9},{1... | collective-permute-start | bytes 393224 | tf_op jit(solution)/shard_map/ppermute | solution.py:20
  7.0 0.8 and_select_fusion.3
  7.7 0.7 slice_bitcast_fusion.4
  8.8 1.6 %fusion.4 = bf16[16,8,5120]{2,1,0:T(8,128)(2,1)} fusion(bf16[1,128,5120]{2,1,0:T(8,128)(2,1)S(1)} %copy-done, s32[128]{0:T(128)S(1)} %fusion.78, s32[16,8]{1,0:T(8,128)S(1)} %multiply_add_fusion.1), kind=kOutput, calls=%fused_computation.5 | convolution fusion | flops 167788544 | bytes 2622464 | tf_op jit(solution)/shard_map/dot_general | solution.py:269
  10.4 3.8 %all-to-all-start = ((bf16[16,8,5120]{2,1,0:T(8,128)(2,1)}), bf16[16,8,5120]{2,1,0:T(8,128)(2,1)S(1)}, u32[]{:S(2)}, u32[]{:S(2)}) async-start(bf16[16,8,5120]{2,1,0:T(8,128)(2,1)} %fusion.4), calls=%async_computation | async-start | bytes 2621440 | tf_op jit(solution)/shard_map/all_to_all | solution.py:270
  16.0 0.7 constant_dynamic-update-slice_fusion.4
  17.5 1.8 %collective-permute-start.3 = (bf16[256,1024]{1,0:T(8,128)(2,1)S(1)}, bf16[256,1024]{1,0:T(8,128)(2,1)S(1)}, u32[]{:S(2)}, u32[]{:S(2)}) collective-permute-start(bf16[256,1024]{1,0:T(8,128)(2,1)S(1)} %pad_maximum_fusion), channel_id=1, source_target_pairs={{0,2},{1,3},{2,0},{3,1},{4,6},{5,7},{6,4},{7,5},{8,10},{9,11},{10,... | collective-permute-start | bytes 1572872 | tf_op jit(solution)/shard_map/ppermute | solution.py:14
  19.2 0.7 constant_dynamic-update-slice_fusion.3
  19.9 0.7 constant_dynamic-update-slice_fusion.2
  20.6 0.7 constant_dynamic-update-slice_fusion.1
  21.2 21.3 %collective-permute-done.3 = bf16[256,1024]{1,0:T(8,128)(2,1)S(1)} collective-permute-done((bf16[256,1024]{1,0:T(8,128)(2,1)S(1)}, bf16[256,1024]{1,0:T(8,128)(2,1)S(1)}, u32[]{:S(2)}, u32[]{:S(2)}) %collective-permute-start.3) | collective-permute-done | bytes 524320 | tf_op jit(solution)/shard_map/ppermute | solution.py:14
  42.5 0.8 constant_dynamic-update-slice_fusion
  44.0 1.1 copy-done.1
  46.2 1.9 %fusion = bf16[128,1024]{1,0:T(8,128)(2,1)S(1)} fusion(s32[1024]{0:T(1024)S(1)} %fusion.65, f32[128,1024]{1,0:T(8,128)S(1)} %copy.39, bf16[128,5120]{1,0:T(8,128)(2,1)} %copy-done.1, f32[128]{0:T(128)S(1)} %add_rsqrt_fusion.1, f32[128]{0:T(128)S(1)} %broadcast_multiply_fusion), kind=kOutput, calls=%fused_computation.1 | convolution fusion | flops 270139392 | bytes 1053696 | tf_op jit(solution)/shard_map/dot_general | solution.py:282
  48.2 1.6 %fusion.39 = f32[128,1024]{1,0:T(8,128)S(1)} fusion(bf16[512,1024]{1,0:T(8,128)(2,1)} %collective-permute-done.4, bf16[128,1024]{1,0:T(8,128)(2,1)S(1)} %fusion), kind=kOutput, calls=%fused_computation.54 | convolution fusion | flops 134217728 | bytes 1703936 | tf_op jit(solution)/shard_map/dot_general | solution.py:286
  49.8 1.4 %multiply_reduce_fusion = (f32[128]{0:T(128)S(1)}, f32[128,1024]{1,0:T(8,128)S(1)}) fusion(f32[128,1024]{1,0:T(8,128)S(1)} %fusion.39, bf16[512,1024]{1,0:T(8,128)(2,1)S(1)} %copy-done.3, bf16[128,1024]{1,0:T(8,128)(2,1)S(1)} %fusion, bf16[128,5120]{1,0:T(8,128)(2,1)} %copy-done.1), kind=kOutput, calls=%fused_computation.27 | convolution fusion | flops 135135104 | bytes 2490880 | tf_op jit(solution)/shard_map/dot_general | solution.py:284
  51.5 1.5 %fusion.36 = bf16[512,1024]{1,0:T(8,128)(2,1)} fusion(s32[128]{0:T(128)S(1)} %get-tuple-element.6, s32[128]{0:T(128)S(1)} %get-tuple-element.5, f32[128,1024]{1,0:T(8,128)S(1)} %get-tuple-element.21, f32[128]{0:T(128)S(1)} %add_rsqrt_fusion), kind=kOutput, calls=%fused_computation.52 | convolution fusion | flops 134676480 | bytes 1574400 | tf_op jit(solution)/shard_map/dot_general | solution.py:302
  53.0 55.4 %expert_exchange.1 = bf16[16,32,1024]{2,1,0:T(8,128)(2,1)} custom-call(bf16[16,32,1024]{2,1,0:T(8,128)(2,1)} %bitcast.74, bf16[1024,512]{1,0:T(8,128)(2,1)} %bitcast.83, bf16[1024,512]{1,0:T(8,128)(2,1)} %bitcast.85, bf16[512,1024]{1,0:T(8,128)(2,1)} %bitcast.87, bf16[1024,512]{1,0:T(8,128)(2,1)} %collective-permute-done.5.refs_3_, ...), custom_call_target="tpu_custom_call" | custom-call | flops 3221225472 | bytes 8388608 | tf_op jit(solution)/shard_map/expert_exchange/pallas_call | solution.py:198
  108.4 1.7 %convolution_multiply_fusion = f32[128,1024]{1,0:T(8,128)S(1)} fusion(bf16[512,1024]{1,0:T(8,128)(2,1)} %bitcast.71, f32[128]{0:T(128)S(1)} %get-tuple-element.15, s32[128]{0:T(128)S(1)} %get-tuple-element.6), kind=kOutput, calls=%fused_computation.9 | convolution fusion | flops 134414336 | bytes 1573888 | tf_op jit(solution)/shard_map/dot_general | solution.py:309
  110.5 1.5 %collective-permute-start.8 = (bf16[1,128,1024]{2,1,0:T(8,128)(2,1)S(1)}, bf16[1,128,1024]{2,1,0:T(8,128)(2,1)S(1)}, u32[]{:S(2)}, u32[]{:S(2)}) collective-permute-start(bf16[1,128,1024]{2,1,0:T(8,128)(2,1)S(1)} %fusion.12), channel_id=1, source_target_pairs={{16,0},{0,16},{17,1},{1,17},{18,2},{2,18},{19,3},{3,19},{20,4},{4,... | collective-permute-start | bytes 786440 | tf_op jit(solution)/shard_map/ppermute | solution.py:20
  112.0 7.5 %collective-permute-done.8 = bf16[1,128,1024]{2,1,0:T(8,128)(2,1)S(1)} collective-permute-done((bf16[1,128,1024]{2,1,0:T(8,128)(2,1)S(1)}, bf16[1,128,1024]{2,1,0:T(8,128)(2,1)S(1)}, u32[]{:S(2)}, u32[]{:S(2)}) %collective-permute-start.8) | collective-permute-done | bytes 262176 | tf_op jit(solution)/shard_map/ppermute | solution.py:20
  119.6 0.7 copy.61
  (72 shorter events, 5.2 us)
Async XLA Ops:
  0.0 8.8 %copy-start = (bf16[1,128,5120]{2,1,0:T(8,128)(2,1)S(1)}, bf16[1,128,5120]{2,1,0:T(8,128)(2,1)}, u32[]{:S(2)}) copy-start(bf16[1,128,5120]{2,1,0:T(8,128)(2,1)} %param.10) | copy-start | bytes 3932164
  0.0 17.1 %collective-permute-start = (bf16[64,1024]{1,0:T(8,128)(2,1)}, bf16[64,1024]{1,0:T(8,128)(2,1)S(1)}, u32[]{:S(2)}, u32[]{:S(2)}) collective-permute-start(bf16[64,1024]{1,0:T(8,128)(2,1)} %bitcast.76), channel_id=1, source_target_pairs={{12,0},{13,1},{14,2},{15,3},{0,4},{1,5},{2,6},{3,7},{4,8},{5,9},{6... | collective-permute-start | bytes 393224 | tf_op jit(solution)/shard_map/ppermute | solution.py:20
  3.0 14.4 %collective-permute-start.1 = (bf16[64,1024]{1,0:T(8,128)(2,1)}, bf16[64,1024]{1,0:T(8,128)(2,1)S(1)}, u32[]{:S(2)}, u32[]{:S(2)}) collective-permute-start(bf16[64,1024]{1,0:T(8,128)(2,1)} %bitcast.77), channel_id=1, source_target_pairs={{8,0},{9,1},{10,2},{11,3},{12,4},{13,5},{14,6},{15,7},{0,8},{1,9},... | collective-permute-start | bytes 393224 | tf_op jit(solution)/shard_map/ppermute | solution.py:20
  5.6 11.8 %collective-permute-start.2 = (bf16[64,1024]{1,0:T(8,128)(2,1)}, bf16[64,1024]{1,0:T(8,128)(2,1)S(1)}, u32[]{:S(2)}, u32[]{:S(2)}) collective-permute-start(bf16[64,1024]{1,0:T(8,128)(2,1)} %bitcast.78), channel_id=1, source_target_pairs={{4,0},{5,1},{6,2},{7,3},{8,4},{9,5},{10,6},{11,7},{12,8},{13,9},{1... | collective-permute-start | bytes 393224 | tf_op jit(solution)/shard_map/ppermute | solution.py:20
  10.4 4.4 %copy-start.8 = (s32[1,1,4]{2,1,0:T(1,128)S(1)}, s32[1,1,4]{2,1,0:T(1,128)}, u32[]{:S(2)}) copy-start(s32[1,1,4]{2,1,0:T(1,128)} %param.12) | copy-start | bytes 52
  10.4 4.7 %copy-start.7 = (s32[1,1,4]{2,1,0:T(1,128)S(1)}, s32[1,1,4]{2,1,0:T(1,128)}, u32[]{:S(2)}) copy-start(s32[1,1,4]{2,1,0:T(1,128)} %param.13) | copy-start | bytes 52
  10.4 4.7 %copy-start.6 = (s32[1,128,2]{1,2,0:T(2,128)S(1)}, s32[1,128,2]{1,2,0:T(2,128)}, u32[]{:S(2)}) copy-start(s32[1,128,2]{1,2,0:T(2,128)} %param.14) | copy-start | bytes 3076
  10.4 5.5 %copy-start.4 = (bf16[1,64,1024]{2,1,0:T(8,128)(2,1)S(1)}, bf16[1,64,1024]{2,1,0:T(8,128)(2,1)}, u32[]{:S(2)}) copy-start(bf16[1,64,1024]{2,1,0:T(8,128)(2,1)} %param.15) | copy-start | bytes 393220
  10.4 32.9 %all-to-all-start = ((bf16[16,8,5120]{2,1,0:T(8,128)(2,1)}), bf16[16,8,5120]{2,1,0:T(8,128)(2,1)S(1)}, u32[]{:S(2)}, u32[]{:S(2)}) async-start(bf16[16,8,5120]{2,1,0:T(8,128)(2,1)} %fusion.4), calls=%async_computation | async-start | bytes 2621440 | tf_op jit(solution)/shard_map/all_to_all | solution.py:270
  14.3 38.7 %collective-permute-start.5 = (bf16[1024,512]{1,0:T(8,128)(2,1)}, bf16[1024,512]{1,0:T(8,128)(2,1)}, u32[]{:S(2)}, u32[]{:S(2)}) collective-permute-start(bf16[1024,512]{1,0:T(8,128)(2,1)} %bitcast.82), channel_id=1, source_target_pairs={{0,1},{1,0},{2,3},{3,2},{4,5},{5,4},{6,7},{7,6},{8,9},{9,8},{10,11... | collective-permute-start | bytes 3145736 | tf_op jit(solution)/shard_map/ppermute | solution.py:14
  14.6 38.4 %collective-permute-start.6 = (bf16[1024,512]{1,0:T(8,128)(2,1)}, bf16[1024,512]{1,0:T(8,128)(2,1)}, u32[]{:S(2)}, u32[]{:S(2)}) collective-permute-start(bf16[1024,512]{1,0:T(8,128)(2,1)} %bitcast.84), channel_id=1, source_target_pairs={{0,1},{1,0},{2,3},{3,2},{4,5},{5,4},{6,7},{7,6},{8,9},{9,8},{10,11... | collective-permute-start | bytes 3145736 | tf_op jit(solution)/shard_map/ppermute | solution.py:14
  17.1 35.9 %collective-permute-start.7 = (bf16[512,1024]{1,0:T(8,128)(2,1)}, bf16[512,1024]{1,0:T(8,128)(2,1)}, u32[]{:S(2)}, u32[]{:S(2)}) collective-permute-start(bf16[512,1024]{1,0:T(8,128)(2,1)} %bitcast.86), channel_id=1, source_target_pairs={{0,1},{1,0},{2,3},{3,2},{4,5},{5,4},{6,7},{7,6},{8,9},{9,8},{10,11... | collective-permute-start | bytes 3145736 | tf_op jit(solution)/shard_map/ppermute | solution.py:14
  17.5 25.1 %collective-permute-start.3 = (bf16[256,1024]{1,0:T(8,128)(2,1)S(1)}, bf16[256,1024]{1,0:T(8,128)(2,1)S(1)}, u32[]{:S(2)}, u32[]{:S(2)}) collective-permute-start(bf16[256,1024]{1,0:T(8,128)(2,1)S(1)} %pad_maximum_fusion), channel_id=1, source_target_pairs={{0,2},{1,3},{2,0},{3,1},{4,6},{5,7},{6,4},{7,5},{8,10},{9,11},{10,... | collective-permute-start | bytes 1572872 | tf_op jit(solution)/shard_map/ppermute | solution.py:14
  43.4 4.8 %collective-permute-start.4 = (bf16[512,1024]{1,0:T(8,128)(2,1)}, bf16[512,1024]{1,0:T(8,128)(2,1)}, u32[]{:S(2)}, u32[]{:S(2)}) collective-permute-start(bf16[512,1024]{1,0:T(8,128)(2,1)} %constant_dynamic-update-slice_fusion), channel_id=1, source_target_pairs={{0,1},{1,0},{2,3},{3,2},{4,5},{5,4},{6,7},{7,6},{8,9},{9,8},{10,11... | collective-permute-start | bytes 3145736 | tf_op jit(solution)/shard_map/ppermute | solution.py:14
  43.9 1.1 copy-start.1
  48.2 1.6 %copy-start.3 = (bf16[512,1024]{1,0:T(8,128)(2,1)S(1)}, bf16[512,1024]{1,0:T(8,128)(2,1)}, u32[]{:S(2)}) copy-start(bf16[512,1024]{1,0:T(8,128)(2,1)} %constant_dynamic-update-slice_fusion) | copy-start | bytes 3145732
  49.8 1.4 %copy-start.5 = (bf16[1,1024,8]{1,2,0:T(8,128)(2,1)S(1)}, bf16[1,1024,8]{1,2,0:T(8,128)(2,1)}, u32[]{:S(2)}) copy-start(bf16[1,1024,8]{1,2,0:T(8,128)(2,1)} %param.16) | copy-start | bytes 49156
  108.4 1.7 %copy-start.2 = (bf16[16,32,1024]{2,1,0:T(8,128)(2,1)S(1)}, bf16[16,32,1024]{2,1,0:T(8,128)(2,1)}, u32[]{:S(2)}) copy-start(bf16[16,32,1024]{2,1,0:T(8,128)(2,1)} %expert_exchange.1) | copy-start | bytes 3145732
  110.5 9.1 %collective-permute-start.8 = (bf16[1,128,1024]{2,1,0:T(8,128)(2,1)S(1)}, bf16[1,128,1024]{2,1,0:T(8,128)(2,1)S(1)}, u32[]{:S(2)}, u32[]{:S(2)}) collective-permute-start(bf16[1,128,1024]{2,1,0:T(8,128)(2,1)S(1)} %fusion.12), channel_id=1, source_target_pairs={{16,0},{0,16},{17,1},{1,17},{18,2},{2,18},{19,3},{3,19},{20,4},{4,... | collective-permute-start | bytes 786440 | tf_op jit(solution)/shard_map/ppermute | solution.py:20
